TPU v7x, 32 devices: a whole 2x2x4 slice. The times are simulated.
32 devices in a mesh: age: 8 (over y, x, core), box: 4 (over z).
Axes of the slice: x: 2, y: 2, z: 4, core: 2. Of those that a mesh axis runs over, the one named last changes fastest.
Arguments:
- position: float32 [3, 131072], P(None, ('age', 'box')), may hold values from -6 to 6
- strength: float32 [3, 131072], P(None, ('age', 'box')), may hold values from -6 to 6
- node_box: int32 [131072], P(('age', 'box')), may hold values from 0 to 1023, as said below
- box_order: int32 [1024], P(('age', 'box')), may hold values from 0 to 1023, as said below
- box_center: float32 [3, 1024], P(None, ('age', 'box')), may hold values from -6 to 6
- near_list: int32 [1024, 4], P(('age', 'box')), may hold values from -1 to 1023, as said below
- m2l_source: int32 [1024, 32], P(('age', 'box')), may hold values from 0 to 1023
- m2l_type: int32 [1024, 32], P(('age', 'box')), may hold values from 0 to 15
- basis_dir: float32 [3, 256], replicated, may hold values from -3.5 to 3.5
- basis_freq: float32 [3, 256], replicated, may hold values from -6 to 6
- basis_phase: float32 [256], replicated, may hold values from -3.140625 to 3.140625
- translation: bfloat16 [16, 256, 256], replicated, may hold values from -0.0012207031 to 0.0012207031
Outputs:
- velocity: float32 [3, 131072], P(None, ('age', 'box'))
Inputs may be any that keep to these rules, and one draw needn't show every extreme that they name: box_order is a permutation of the box ids. `node_box`: every entry is a box id. Of the 4096 nodes of one device (aligned blocks of 4096 entries), at most 256 lie in the boxes held by any one device, that is the boxes box_order[g * 32] to box_order[g * 32 + 31]; in every draw some device holds the boxes of exactly 256 nodes of every device. Over all nodes, at most 256 lie in any one box, and in every draw some box holds exactly 256. `near_list`: row p lists box_order[p] first, then distinct other boxes held by the same device as position p, then -1 padding. `m2l_source`: entries are box ids; repeats may occur.
All inputs are finite; a program needn't handle non-finite values.
Results may differ from a plain program's by a relative error of at most 0.0025.
Values may be sent and summed in bfloat16 or wider, within the bound.
A program may use at most 64 MiB of HBM per device.

v0:
```python
import functools

import jax
import jax.numpy as jnp
import numpy as np
from jax import lax
from jax.experimental import pallas as pl
from jax.experimental.pallas import tpu as pltpu
from jax.sharding import PartitionSpec as P

AXES = ("age", "box")
core_square = 0.01
inv_four_pi = 0.07957747154594767
inv_two_pi = 0.15915494309189535
LANES = 128
VMEM_LIMIT = 48 * 1024 * 1024


def cos_coefficients(degree):
    nodes = np.cos(np.pi * (np.arange(64) + 0.5) / 64)
    w = 0.125 * (nodes + 1.0)
    fit = np.polynomial.chebyshev.Chebyshev.fit(
        w, np.cos(2 * np.pi * np.sqrt(w)), degree, domain=[0, 0.25]
    )
    return [float(c) for c in fit.convert(kind=np.polynomial.Polynomial).coef]


COS_COEF = cos_coefficients(8)


def cos_turns(turns):
    v = turns - jnp.round(turns)
    w = v * v
    acc = jnp.full_like(w, COS_COEF[-1])
    for c in COS_COEF[-2::-1]:
        acc = acc * w + c
    return acc


def gather_body(n_box, n, x_ref, o_ref, send_sem, recv_sem):
    me = lax.axis_index("age") * n_box + lax.axis_index("box")
    barrier = pltpu.get_barrier_semaphore()

    def peer(d):
        other = lax.rem(me + d, n)
        return {"age": other // n_box, "box": lax.rem(other, n_box)}

    def greet(d, carry):
        pl.semaphore_signal(
            barrier, inc=1, device_id=peer(d), device_id_type=pl.DeviceIdType.MESH
        )
        return carry

    lax.fori_loop(1, n, greet, 0)
    o_ref[me] = x_ref[...]
    pl.semaphore_wait(barrier, n - 1)

    def copy(d):
        return pltpu.make_async_remote_copy(
            src_ref=x_ref,
            dst_ref=o_ref.at[me],
            send_sem=send_sem.at[d - 1],
            recv_sem=recv_sem.at[d - 1],
            device_id=peer(d),
            device_id_type=pl.DeviceIdType.MESH,
        )

    def send(d, carry):
        copy(d).start()
        return carry

    def finish(d, carry):
        copy(d).wait()
        return carry

    lax.fori_loop(1, n, send, 0)
    lax.fori_loop(1, n, finish, 0)


def gather_blocks(x, n_box, n, collective_id):
    return pl.pallas_call(
        functools.partial(gather_body, n_box, n),
        out_shape=jax.ShapeDtypeStruct((n,) + x.shape, x.dtype),
        in_specs=[pl.BlockSpec(memory_space=pltpu.VMEM)],
        out_specs=pl.BlockSpec(memory_space=pltpu.VMEM),
        scratch_shapes=[
            pltpu.SemaphoreType.DMA((n - 1,)),
            pltpu.SemaphoreType.DMA((n - 1,)),
        ],
        compiler_params=pltpu.CompilerParams(
            collective_id=collective_id, has_side_effects=True
        ),
    )(x)


def lanes_to_rows(tile):
    padded = jnp.concatenate([tile, jnp.zeros((LANES - tile.shape[0], LANES), tile.dtype)], axis=0)
    return padded.T


def fill_rows(src_ref, rows_ref, count):
    def step(i, carry):
        at = pl.multiple_of(i * LANES, LANES)
        rows_ref[pl.ds(at, LANES), :] = lanes_to_rows(src_ref[:, pl.ds(at, LANES)])
        return carry

    lax.fori_loop(0, count // LANES, step, 0)


def take_lanes(rows_ref, out_ref, count):
    def step(i, carry):
        at = pl.multiple_of(i * LANES, LANES)
        out_ref[:, pl.ds(at, LANES)] = rows_ref[pl.ds(at, LANES), :].T[: out_ref.shape[0]]
        return carry

    lax.fori_loop(0, count // LANES, step, 0)


def zero_rows(ref):
    def step(i, carry):
        at = pl.multiple_of(i * 8, 8)
        ref[pl.ds(at, 8), :] = jnp.zeros((8, LANES), jnp.float32)
        return carry

    lax.fori_loop(0, ref.shape[0] // 8, step, 0, unroll=8)


def scatter_rows(idx_ref, src_ref, dst_ref, count):
    def step(i, carry):
        at = pl.multiple_of(i * 16, 16)
        block = src_ref[pl.ds(at, 16), :]
        for u in range(16):
            dst_ref[pl.ds(idx_ref[at + u], 1), :] = block[u : u + 1, :]
        return carry

    lax.fori_loop(0, count // 16, step, 0)


def gather_rows(idx_ref, src_ref, dst_ref, count):
    def step(i, carry):
        at = pl.multiple_of(i * 16, 16)
        rows = [src_ref[pl.ds(idx_ref[at + u], 1), :] for u in range(16)]
        dst_ref[pl.ds(at, 16), :] = jnp.concatenate(rows, axis=0)
        return carry

    lax.fori_loop(0, count // 16, step, 0)


def spread_body(idx_ref, x_ref, out_ref, rows, placed):
    fill_rows(x_ref, rows, x_ref.shape[1])
    zero_rows(placed)
    scatter_rows(idx_ref, rows, placed, x_ref.shape[1])
    take_lanes(placed, out_ref, out_ref.shape[1])


def group_body(idx_ref, x_ref, out_ref, rows):
    fill_rows(x_ref, rows, x_ref.shape[1])
    zero_rows(out_ref)
    scatter_rows(idx_ref, rows, out_ref, x_ref.shape[1])


def ungroup_body(idx_ref, x_ref, out_ref, rows):
    gather_rows(idx_ref, x_ref, rows, out_ref.shape[1])
    take_lanes(rows, out_ref, out_ref.shape[1])


def collect_body(idx_ref, x_ref, out_ref, src, rows):
    fill_rows(x_ref, src, x_ref.shape[1])
    gather_rows(idx_ref, src, rows, out_ref.shape[1])
    take_lanes(rows, out_ref, out_ref.shape[1])


def permute_call(body, idx, x, out_shape, scratch_rows):
    return pl.pallas_call(
        body,
        out_shape=jax.ShapeDtypeStruct(out_shape, jnp.float32),
        in_specs=[
            pl.BlockSpec(memory_space=pltpu.SMEM),
            pl.BlockSpec(memory_space=pltpu.VMEM),
        ],
        out_specs=pl.BlockSpec(memory_space=pltpu.VMEM),
        scratch_shapes=[pltpu.VMEM((r, LANES), jnp.float32) for r in scratch_rows],
        compiler_params=pltpu.CompilerParams(vmem_limit_bytes=VMEM_LIMIT),
    )(idx, x)


def ranks(key, kinds):
    count = key.shape[0]
    blocks = count // LANES
    hits = (key[None, :] == jnp.arange(kinds, dtype=jnp.int32)[:, None]).reshape(
        kinds, blocks, LANES
    )
    hits16 = hits.astype(jnp.bfloat16)
    lane = np.arange(LANES)
    before = jnp.asarray(lane[:, None] < lane[None, :], jnp.bfloat16)
    inside = jnp.dot(
        hits16.reshape(kinds * blocks, LANES), before, preferred_element_type=jnp.float32
    ).reshape(kinds, blocks, LANES)
    totals = jnp.sum(hits.astype(jnp.float32), axis=2)
    block = np.arange(blocks)
    base = jnp.dot(
        totals.astype(jnp.bfloat16),
        jnp.asarray(block[:, None] < block[None, :], jnp.bfloat16),
        preferred_element_type=jnp.float32,
    )
    rank = jnp.sum(jnp.where(hits, inside + base[:, :, None], 0.0), axis=0)
    return rank.reshape(count).astype(jnp.int32)


def split16(x):
    high = x.astype(jnp.bfloat16)
    return high, (x - high.astype(jnp.float32)).astype(jnp.bfloat16)


def box_body(center_ref, rows_ref, basis_ref, block_ref, wave_ref, lanes_ref, parts_ref):
    b = pl.program_id(0)
    count = rows_ref.shape[0]
    cx, cy, cz = center_ref[0, b], center_ref[1, b], center_ref[2, b]
    fx, fy, fz = basis_ref[0:1, :], basis_ref[1:2, :], basis_ref[2:3, :]
    phase = basis_ref[3:4, :]
    ux, uy, uz = basis_ref[4:5, :], basis_ref[5:6, :], basis_ref[6:7, :]
    chunk = 32
    total = jnp.zeros((8, fx.shape[1]), jnp.float32)
    for c in range(count // chunk):
        r = rows_ref[c * chunk : (c + 1) * chunk, :]
        turns = (
            fx * (r[:, 0:1] - cx) + fy * (r[:, 1:2] - cy) + fz * (r[:, 2:3] - cz) + phase
        )
        wave = cos_turns(turns)
        wave_ref[c * chunk : (c + 1) * chunk, :] = wave
        charge = ux * r[:, 3:4] + uy * r[:, 4:5] + uz * r[:, 5:6]
        product = charge * wave
        for s in range(chunk // 8):
            total = total + product[s * 8 : (s + 1) * 8]
    block_ref[0] = jnp.sum(total, axis=0, keepdims=True)
    lanes = jnp.concatenate(
        [rows_ref[i * LANES : (i + 1) * LANES, :].T[:8] for i in range(count // LANES)], axis=1
    )
    lanes_ref[0] = lanes
    x, y, z = lanes[0:1], lanes[1:2], lanes[2:3]
    sx, sy, sz = lanes[3:4], lanes[4:5], lanes[5:6]
    zero = jnp.zeros_like(x)
    table = jnp.concatenate(
        [sx, sy, sz, zero, sy * z - sz * y, sz * x - sx * z, sx * y - sy * x, zero], axis=0
    )
    high = table.astype(jnp.bfloat16).astype(jnp.float32)
    parts_ref[0] = jnp.concatenate([high, table - high], axis=0).astype(jnp.bfloat16)


def box_call(center, rows, basis, boxes, per_box):
    coef = basis.shape[1]
    return pl.pallas_call(
        box_body,
        grid=(boxes,),
        out_shape=(
            jax.ShapeDtypeStruct((boxes, 1, coef), jnp.float32),
            jax.ShapeDtypeStruct((boxes * per_box, coef), jnp.float32),
            jax.ShapeDtypeStruct((boxes, 8, per_box), jnp.float32),
            jax.ShapeDtypeStruct((boxes, 16, per_box), jnp.bfloat16),
        ),
        in_specs=[
            pl.BlockSpec(memory_space=pltpu.SMEM),
            pl.BlockSpec((per_box, LANES), lambda b: (b, 0)),
            pl.BlockSpec((8, coef), lambda b: (0, 0)),
        ],
        out_specs=(
            pl.BlockSpec((1, 1, coef), lambda b: (b, 0, 0)),
            pl.BlockSpec((per_box, coef), lambda b: (b, 0)),
            pl.BlockSpec((1, 8, per_box), lambda b: (b, 0, 0)),
            pl.BlockSpec((1, 16, per_box), lambda b: (b, 0, 0)),
        ),
        compiler_params=pltpu.CompilerParams(vmem_limit_bytes=VMEM_LIMIT),
    )(center, rows, basis)


def velocity_body(
    near_ref, rows_ref, lanes_ref, parts_ref, wave_ref, exp_ref, dir_ref, out_ref, acc
):
    b = pl.program_id(0)
    per_box = wave_ref.shape[0]
    lanes = lanes_ref[b]
    tx, ty, tz = lanes[0:1], lanes[1:2], lanes[2:3]
    acc[...] = jnp.zeros_like(acc)
    chunk = 64
    for v in range(near_ref.shape[1]):
        j = near_ref[b, v]

        @pl.when(j >= 0)
        def _():
            start = j * per_box
            pieces = []
            for c in range(per_box // chunk):
                at = pl.multiple_of(start + c * chunk, chunk)
                s = rows_ref[pl.ds(at, chunk), :]
                dx = tx - s[:, 0:1]
                dy = ty - s[:, 1:2]
                dz = tz - s[:, 2:3]
                r = lax.rsqrt(dx * dx + dy * dy + dz * dz + core_square)
                pieces.append((r * r * r).astype(jnp.bfloat16))
            factor = jnp.concatenate(pieces, axis=0)
            acc[...] += jnp.dot(parts_ref[j], factor, preferred_element_type=jnp.float32)

    sums = acc[...]
    sums = sums[0:8] + sums[8:16]
    ax, ay, az = sums[0:1], sums[1:2], sums[2:3]
    nx = ay * tz - az * ty - sums[4:5]
    ny = az * tx - ax * tz - sums[5:6]
    nz = ax * ty - ay * tx - sums[6:7]
    near = jnp.concatenate([nx, ny, nz, jnp.zeros((5, per_box), jnp.float32)], axis=0)
    near = near * inv_four_pi
    high, low = split16(wave_ref[...] * exp_ref[0])
    table = dir_ref[...]
    both = jnp.dot(high, table, preferred_element_type=jnp.float32)
    both = both + jnp.dot(low, table, preferred_element_type=jnp.float32)
    far = both[:, :LANES] + both[:, LANES:]
    for i in range(per_box // LANES):
        out_ref[i * LANES : (i + 1) * LANES, :] = far[
            i * LANES : (i + 1) * LANES
        ] + lanes_to_rows(near[:, i * LANES : (i + 1) * LANES])


def velocity_call(near, rows, lanes, parts, wave, exps, table, boxes, per_box):
    coef = wave.shape[1]
    return pl.pallas_call(
        velocity_body,
        grid=(boxes,),
        out_shape=jax.ShapeDtypeStruct((boxes * per_box, LANES), jnp.float32),
        in_specs=[
            pl.BlockSpec(memory_space=pltpu.SMEM),
            pl.BlockSpec(memory_space=pltpu.VMEM),
            pl.BlockSpec(memory_space=pltpu.VMEM),
            pl.BlockSpec(memory_space=pltpu.VMEM),
            pl.BlockSpec((per_box, coef), lambda b: (b, 0)),
            pl.BlockSpec((1, 1, coef), lambda b: (b, 0, 0)),
            pl.BlockSpec(memory_space=pltpu.VMEM),
        ],
        out_specs=pl.BlockSpec((per_box, LANES), lambda b: (b, 0)),
        scratch_shapes=[pltpu.VMEM((16, per_box), jnp.float32)],
        compiler_params=pltpu.CompilerParams(vmem_limit_bytes=VMEM_LIMIT),
    )(near, rows, lanes, parts, wave, exps, table)


def per_device(
    n_box,
    groups,
    position,
    strength,
    node_box,
    box_order,
    box_center,
    near_list,
    m2l_source,
    m2l_type,
    basis_dir,
    basis_freq,
    basis_phase,
    translation,
):
    node_count = position.shape[1]
    box_local = box_order.shape[0]
    slots_total = 2 * node_count
    per_peer = slots_total // groups
    per_box = slots_total // box_local
    coef = basis_phase.shape[0]
    kind_count = translation.shape[0]
    box_total = groups * box_local

    padded_order = jnp.pad(box_order, (0, LANES - box_local)).reshape(1, LANES)
    all_order = gather_blocks(padded_order, n_box, groups, 0)[:, 0, :box_local].reshape(-1)

    node_slot = jnp.sum(
        jnp.where(
            node_box[None, :] == all_order[:, None],
            jnp.arange(box_total, dtype=jnp.int32)[:, None],
            0,
        ),
        axis=0,
    )
    owner = node_slot // box_local
    label = (node_slot - owner * box_local + 1).astype(jnp.float32)
    send_at = owner * per_peer + ranks(owner, groups)
    fields = jnp.concatenate(
        [position, strength, label[None, :], jnp.zeros((1, node_count), jnp.float32)], axis=0
    )
    payload = permute_call(
        spread_body, send_at, fields, (8, slots_total), (node_count, slots_total)
    )
    got = lax.all_to_all(payload, AXES, split_axis=1, concat_axis=1, tiled=True)

    hit_source = (m2l_source[:, :, None] == all_order[None, None, :]).astype(jnp.bfloat16)
    kind_hits = (
        m2l_type[:, :, None] == jnp.arange(kind_count, dtype=jnp.int32)[None, None, :]
    ).astype(jnp.bfloat16)
    list_counts = jnp.einsum(
        "jlt,jlb->tjb", kind_hits, hit_source, preferred_element_type=jnp.float32
    )
    list_counts = list_counts.astype(jnp.bfloat16).reshape(kind_count * box_local, box_total)
    near_local = jnp.sum(
        jnp.where(
            near_list[:, :, None] == box_order[None, None, :],
            jnp.arange(1, box_local + 1, dtype=jnp.int32)[None, None, :],
            0,
        ),
        axis=2,
    ) - 1

    got_label = got[6].astype(jnp.int32) - 1
    live = got_label >= 0
    tile_at = jnp.where(
        live, got_label * per_box + ranks(got_label, box_local), slots_total
    )
    rows = permute_call(group_body, tile_at, got, (slots_total + 8, LANES), (slots_total,))
    basis = jnp.concatenate(
        [
            basis_freq * inv_two_pi,
            basis_phase[None, :] * inv_two_pi,
            basis_dir,
            jnp.zeros((1, coef), jnp.float32),
        ],
        axis=0,
    )
    sums, wave, lanes, parts = box_call(box_center, rows, basis, box_local, per_box)
    local_blocks = sums.reshape(box_local, coef).astype(jnp.bfloat16)
    all_blocks = gather_blocks(local_blocks, n_box, groups, 1).reshape(box_total, coef)
    mixed = jnp.dot(list_counts, all_blocks, preferred_element_type=jnp.float32)
    mixed = mixed.astype(jnp.bfloat16).reshape(kind_count, box_local, coef)
    expansions = jnp.einsum(
        "tjc,tkc->jk", mixed, translation, preferred_element_type=jnp.float32
    )
    dir_high, dir_low = split16(basis_dir.T)
    pad = ((0, 0), (0, LANES - 3))
    table = jnp.concatenate([jnp.pad(dir_high, pad), jnp.pad(dir_low, pad)], axis=1)
    vel_rows = velocity_call(
        near_local,
        rows,
        lanes,
        parts,
        wave,
        expansions.reshape(box_local, 1, coef),
        table,
        box_local,
        per_box,
    )
    back = permute_call(
        ungroup_body,
        jnp.minimum(tile_at, slots_total - 1),
        vel_rows,
        (8, slots_total),
        (slots_total,),
    )
    returned = lax.all_to_all(back[:3], AXES, split_axis=1, concat_axis=1, tiled=True)
    returned = jnp.pad(returned, ((0, 5), (0, 0)))
    out = permute_call(
        collect_body, send_at, returned, (8, node_count), (slots_total, node_count)
    )
    return out[:3]


def solution(mesh):
    n_box = mesh.shape["box"]
    groups = mesh.shape["age"] * n_box
    placed = (
        P(None, AXES),
        P(None, AXES),
        P(AXES),
        P(AXES),
        P(None, AXES),
        P(AXES, None),
        P(AXES, None),
        P(AXES, None),
        P(),
        P(),
        P(),
        P(),
    )
    return jax.shard_map(
        functools.partial(per_device, n_box, groups),
        mesh=mesh,
        in_specs=placed,
        out_specs=P(None, AXES),
        check_vma=False,
    )
```

profile of v0, /device:TPU:0, one launch (start us, length us, event | category | flops | bytes accessed | tf_op | source)
XLA Modules:
  0.0 194.1 jit_solution(6638513752860511152)
XLA Ops:
  0.0 1.3 pad_bitcast_fusion.x_ref
  1.3 11.3 %shard_map.154 = s32[32,1,128]{2,1,0:T(1,128)} custom-call(s32[1,128]{1,0:T(1,128)} %pad_bitcast_fusion.x_ref), custom_call_target="tpu_custom_call" | custom-call | tf_op jit(solution)/shard_map/pallas_call | solution.py:81
  12.7 0.8 slice_reduce_fusion
  13.5 3.0 %select_reduce_fusion = s32[4096]{0:T(1024)S(1)} fusion(s32[4096]{0:T(1024)} %param.18, s32[1024]{0:T(1024)S(1)} %eq.87), kind=kLoop, calls=%fused_computation | loop fusion | flops 12578816 | bytes 36864 | tf_op jit(solution)/shard_map/reduce_sum | solution.py:371
  16.5 0.2 convert_reduce_fusion.1
  16.8 0.8 fusion.38
  17.6 1.0 fusion.13
  18.8 0.9 maximum_maximum_fusion.x_ref
  19.8 14.3 %shard_map.155 = f32[8,8192]{1,0:T(8,128)} custom-call(s32[4096]{0:T(1024)S(1)} %fusion.25.idx_ref, f32[8,4096]{1,0:T(8,128)S(1)} %maximum_maximum_fusion.x_ref), custom_call_target="tpu_custom_call" | custom-call | tf_op jit(solution)/shard_map/pallas_call | solution.py:174
  34.0 5.1 %all-to-all-start = ((f32[8,32,256]{2,0,1:T(8,128)}), f32[8,32,256]{2,0,1:T(8,128)S(1)}, u32[]{:S(2)}, u32[]{:S(2)}) async-start(f32[8,32,256]{2,0,1:T(8,128)} %bitcast.5), calls=%async_computation | async-start | bytes 524288 | tf_op jit(solution)/shard_map/all_to_all | solution.py:388
  39.1 0.7 broadcast_multiply_fusion.2
  39.8 0.7 broadcast_multiply_fusion.1
  40.5 0.9 select_reduce_fusion.1
  41.5 0.8 copy.39
  42.4 1.6 fusion.7
  44.0 1.6 copy.37
  45.7 3.6 %all-to-all-done = f32[8,32,256]{2,0,1:T(8,128)S(1)} async-done(((f32[8,32,256]{2,0,1:T(8,128)}), f32[8,32,256]{2,0,1:T(8,128)S(1)}, u32[]{:S(2)}, u32[]{:S(2)}) %all-to-all-start) | async-done | bytes 262176 | tf_op jit(solution)/shard_map/all_to_all | solution.py:388
  49.5 0.4 convert_reduce_fusion
  49.9 0.1 fusion.37
  50.0 0.4 fusion.11
  50.4 16.8 %shard_map.156.rows_ref = f32[8200,128]{1,0:T(8,128)S(1)} custom-call(s32[8192]{0:T(1024)S(1)} %get-tuple-element.16.idx_ref, f32[8,8192]{1,0:T(8,128)S(1)} %bitcast.62), custom_call_target="tpu_custom_call" | custom-call | tf_op jit(solution)/shard_map/pallas_call | solution.py:174
  67.2 18.6 %shard_map.157 = (f32[32,1,256]{2,1,0:T(1,128)S(1)}, f32[8192,256]{1,0:T(8,128)}, f32[32,8,256]{2,1,0:T(8,128)S(1)}, bf16[32,16,256]{2,1,0:T(8,128)(2,1)S(1)}) custom-call(f32[3,32]{1,0:T(4,128)S(1)} %copy-done.2, f32[8200,128]{1,0:T(8,128)S(1)} %shard_map.156.rows_ref, f32[8,256]{1,0:T(8,128)S(1)} %maximum_maximum_fusion.1.basis_ref), custom_call_target="tpu_custom_call" | custom-call | tf_op jit(solution)/shard_map/pallas_call | solution.py:252
  85.8 2.0 %copy-done.1 = f32[8200,128]{1,0:T(8,128)} copy-done((f32[8200,128]{1,0:T(8,128)}, f32[8200,128]{1,0:T(8,128)S(1)}, u32[]{:S(2)}) %copy-start.1) | copy-done | bytes 4198424
  87.8 0.6 copy.44
  88.4 17.7 %shard_map.158 = bf16[32,32,256]{2,1,0:T(8,128)(2,1)} custom-call(bf16[32,256]{1,0:T(8,128)(2,1)} %bitcast.72), custom_call_target="tpu_custom_call" | custom-call | tf_op jit(solution)/shard_map/pallas_call | solution.py:81
  106.2 1.8 convolution_convert_fusion
  108.0 0.7 convolution_bitcast_fusion
  108.7 45.8 %shard_map.159.x_ref = f32[8192,128]{1,0:T(8,128)S(1)} custom-call(s32[32,4]{1,0:T(8,128)S(1)} %broadcast_add_fusion.near_ref, f32[8200,128]{1,0:T(8,128)} %copy-done.1, f32[32,8,256]{2,1,0:T(8,128)S(1)} %get-tuple-element.9.lanes_ref, bf16[32,16,256]{2,1,0:T(8,128)(2,1)S(1)} %get-tuple-element.10.parts_ref, f32[8192,256]{1,0:T(8,128)} %get-tuple-element.11.wave_ref, ...), custom_call_target="tpu_custom_call" | custom-call | tf_op jit(solution)/shard_map/pallas_call | solution.py:324
  154.5 14.6 %shard_map.160 = f32[8,8192]{1,0:T(8,128)S(1)} custom-call(s32[8192]{0:T(1024)S(1)} %get-tuple-element.15.idx_ref, f32[8192,128]{1,0:T(8,128)S(1)} %shard_map.159.x_ref), custom_call_target="tpu_custom_call" | custom-call | tf_op jit(solution)/shard_map/pallas_call | solution.py:174
  169.2 10.1 %all_to_all.23 = f32[3,32,256]{2,0,1:T(4,128)S(1)} all-to-all(f32[3,32,256]{2,0,1:T(4,128)S(1)} %bitcast.66), channel_id=1, replica_groups=mesh['age'=8,'box'=4] {'age','box'}, dimensions={1} | all-to-all | bytes 196608 | tf_op jit(solution)/shard_map/all_to_all | solution.py:451
  179.3 14.1 %shard_map.161 = f32[8,4096]{1,0:T(8,128)S(1)} custom-call(s32[4096]{0:T(1024)S(1)} %fusion.25.idx_ref, f32[8,8192]{1,0:T(8,128)S(1)} %pad.18.x_ref), custom_call_target="tpu_custom_call" | custom-call | tf_op jit(solution)/shard_map/pallas_call | solution.py:174
  193.4 0.7 slice.19
  (29 shorter events, 0.8 us)
Async XLA Ops:
  0.0 108.0 %copy-start = (bf16[16,256,256]{2,1,0:T(8,128)(2,1)S(1)}, bf16[16,256,256]{2,1,0:T(8,128)(2,1)}, u32[]{:S(2)}) copy-start(bf16[16,256,256]{2,1,0:T(8,128)(2,1)} %param.27) | copy-start | bytes 6291460
  0.0 50.0 %copy-start.5 = (bf16[128,128,1]{1,0,2:T(8,128)(2,1)S(1)}, bf16[128,128,1]{1,0,2:T(8,128)(2,1)}, u32[]{:S(2)}) copy-start(bf16[128,128,1]{1,0,2:T(8,128)(2,1)} %constant.60) | copy-start | bytes 98308
  0.0 49.9 %copy-start.3 = (bf16[64,64]{1,0:T(8,128)(2,1)S(1)}, bf16[64,64]{1,0:T(8,128)(2,1)}, u32[]{:S(2)}) copy-start(bf16[64,64]{1,0:T(8,128)(2,1)} %constant.51.clone) | copy-start | bytes 24580
  0.0 45.6 %copy-start.4 = (f32[3,256]{1,0:T(4,128)S(1)}, f32[3,256]{1,0:T(4,128)}, u32[]{:S(2)}) copy-start(f32[3,256]{1,0:T(4,128)} %param.24) | copy-start | bytes 9220
  34.0 15.3 %all-to-all-start = ((f32[8,32,256]{2,0,1:T(8,128)}), f32[8,32,256]{2,0,1:T(8,128)S(1)}, u32[]{:S(2)}, u32[]{:S(2)}) async-start(f32[8,32,256]{2,0,1:T(8,128)} %bitcast.5), calls=%async_computation | async-start | bytes 524288 | tf_op jit(solution)/shard_map/all_to_all | solution.py:388
  44.0 23.3 %copy-start.2 = (f32[3,32]{1,0:T(4,128)S(1)}, f32[3,32]{1,0:T(4,128)}, u32[]{:S(2)}) copy-start(f32[3,32]{1,0:T(4,128)} %center_ref.1) | copy-start | bytes 1156
  85.8 2.0 %copy-start.1 = (f32[8200,128]{1,0:T(8,128)}, f32[8200,128]{1,0:T(8,128)S(1)}, u32[]{:S(2)}) copy-start(f32[8200,128]{1,0:T(8,128)S(1)} %shard_map.156.rows_ref) | copy-start | bytes 12595204
where the time goes:
time: 194 us
  Pallas kernels  153 us (79%)
  blocking collectives  10.1 us (5%)
  local copies, waits for them, and re-layouts  8.13 us (4%)
  other arithmetic  7.26 us (4%)
  matrix products  6.39 us (3%)
  starting transfers between devices  5.11 us (3%)
  waiting for transfers between devices  3.62 us (2%)
    pallas_call x4, Pallas kernels, permute_call(): pl.pallas_call(body, out_shape=jax.ShapeDtypeStruct(out_shape, jnp.float3...  59.8 us
    pallas_call x1, Pallas kernels, velocity_call(): pl.pallas_call(velocity_body, grid=(boxes,), out_shape=jax.ShapeDtypeStru...  45.8 us
    pallas_call x2, Pallas kernels, gather_blocks(): pl.pallas_call(functools.partial(gather_body, n_box, n), out_shape=jax.Sh...  29.1 us
    pallas_call x1, Pallas kernels, box_call(): pl.pallas_call(box_body, grid=(boxes,), out_shape=(jax.ShapeDtypeStruct((...  18.6 us
    all_to_all x1, blocking collectives, per_device(): lax.all_to_all(back[:3], AXES, split_axis=1, concat_axis=1, tiled=True)  10.1 us
    all_to_all x1, starting transfers between devices, per_device(): got = lax.all_to_all(payload, AXES, split_axis=1, concat_axis=1, tiled=True)  5.11 us
  transfers between devices with their start and end apart: 1, of which 1 were waited for; matrix products, arithmetic and copies ran while one was open for 3% of the time, Pallas kernels for 0%

commit v1 on v0

--- a/solution.py
+++ b/solution.py
@@ -25,11 +25,11 @@
     return [float(c) for c in fit.convert(kind=np.polynomial.Polynomial).coef]
 
 
-COS_COEF = cos_coefficients(8)
+COS_COEF = cos_coefficients(6)
 
 
 def cos_turns(turns):
-    v = turns - jnp.round(turns)
+    v = turns - ((turns + 12582912.0) - 12582912.0)
     w = v * v
     acc = jnp.full_like(w, COS_COEF[-1])
     for c in COS_COEF[-2::-1]:
@@ -37,55 +37,80 @@
     return acc
 
 
-def gather_body(n_box, n, x_ref, o_ref, send_sem, recv_sem):
-    me = lax.axis_index("age") * n_box + lax.axis_index("box")
+def gather_body(n_age, n_box, x_ref, o_ref, send_sem, recv_sem):
+    me_age, me_box = lax.axis_index("age"), lax.axis_index("box")
     barrier = pltpu.get_barrier_semaphore()
 
-    def peer(d):
-        other = lax.rem(me + d, n)
-        return {"age": other // n_box, "box": lax.rem(other, n_box)}
-
-    def greet(d, carry):
-        pl.semaphore_signal(
-            barrier, inc=1, device_id=peer(d), device_id_type=pl.DeviceIdType.MESH
-        )
-        return carry
-
-    lax.fori_loop(1, n, greet, 0)
-    o_ref[me] = x_ref[...]
-    pl.semaphore_wait(barrier, n - 1)
-
-    def copy(d):
+    def on_box(d):
+        return {"age": me_age, "box": lax.rem(me_box + d, n_box)}
+
+    def on_age(d):
+        return {"age": lax.rem(me_age + d, n_age), "box": me_box}
+
+    def greet(peer):
+        def step(d, carry):
+            pl.semaphore_signal(
+                barrier, inc=1, device_id=peer(d), device_id_type=pl.DeviceIdType.MESH
+            )
+            return carry
+
+        return step
+
+    lax.fori_loop(1, n_box, greet(on_box), 0)
+    lax.fori_loop(1, n_age, greet(on_age), 0)
+    o_ref[me_age, me_box] = x_ref[...]
+    pl.semaphore_wait(barrier, n_box - 1 + n_age - 1)
+
+    def along_box(d):
         return pltpu.make_async_remote_copy(
             src_ref=x_ref,
-            dst_ref=o_ref.at[me],
+            dst_ref=o_ref.at[me_age, me_box],
             send_sem=send_sem.at[d - 1],
             recv_sem=recv_sem.at[d - 1],
-            device_id=peer(d),
+            device_id=on_box(d),
             device_id_type=pl.DeviceIdType.MESH,
         )
 
-    def send(d, carry):
-        copy(d).start()
-        return carry
-
-    def finish(d, carry):
-        copy(d).wait()
-        return carry
-
-    lax.fori_loop(1, n, send, 0)
-    lax.fori_loop(1, n, finish, 0)
-
-
-def gather_blocks(x, n_box, n, collective_id):
+    def along_age(d):
+        return pltpu.make_async_remote_copy(
+            src_ref=o_ref.at[me_age],
+            dst_ref=o_ref.at[me_age],
+            send_sem=send_sem.at[n_box - 2 + d],
+            recv_sem=recv_sem.at[n_box - 2 + d],
+            device_id=on_age(d),
+            device_id_type=pl.DeviceIdType.MESH,
+        )
+
+    def start(copy):
+        def step(d, carry):
+            copy(d).start()
+            return carry
+
+        return step
+
+    def finish(copy):
+        def step(d, carry):
+            copy(d).wait()
+            return carry
+
+        return step
+
+    lax.fori_loop(1, n_box, start(along_box), 0)
+    lax.fori_loop(1, n_box, finish(along_box), 0)
+    lax.fori_loop(1, n_age, start(along_age), 0)
+    lax.fori_loop(1, n_age, finish(along_age), 0)
+
+
+def gather_blocks(x, n_age, n_box, collective_id):
+    copies = n_age + n_box - 2
     return pl.pallas_call(
-        functools.partial(gather_body, n_box, n),
-        out_shape=jax.ShapeDtypeStruct((n,) + x.shape, x.dtype),
+        functools.partial(gather_body, n_age, n_box),
+        out_shape=jax.ShapeDtypeStruct((n_age, n_box) + x.shape, x.dtype),
         in_specs=[pl.BlockSpec(memory_space=pltpu.VMEM)],
         out_specs=pl.BlockSpec(memory_space=pltpu.VMEM),
         scratch_shapes=[
-            pltpu.SemaphoreType.DMA((n - 1,)),
-            pltpu.SemaphoreType.DMA((n - 1,)),
+            pltpu.SemaphoreType.DMA((copies,)),
+            pltpu.SemaphoreType.DMA((copies,)),
         ],
         compiler_params=pltpu.CompilerParams(
             collective_id=collective_id, has_side_effects=True
@@ -104,7 +129,7 @@
         rows_ref[pl.ds(at, LANES), :] = lanes_to_rows(src_ref[:, pl.ds(at, LANES)])
         return carry
 
-    lax.fori_loop(0, count // LANES, step, 0)
+    lax.fori_loop(0, count // LANES, step, 0, unroll=8)
 
 
 def take_lanes(rows_ref, out_ref, count):
@@ -113,7 +138,7 @@
         out_ref[:, pl.ds(at, LANES)] = rows_ref[pl.ds(at, LANES), :].T[: out_ref.shape[0]]
         return carry
 
-    lax.fori_loop(0, count // LANES, step, 0)
+    lax.fori_loop(0, count // LANES, step, 0, unroll=8)
 
 
 def zero_rows(ref):
@@ -207,44 +232,71 @@
     return rank.reshape(count).astype(jnp.int32)
 
 
-def split16(x):
-    high = x.astype(jnp.bfloat16)
-    return high, (x - high.astype(jnp.float32)).astype(jnp.bfloat16)
+def split16(x, parts):
+    pieces = []
+    for _ in range(parts):
+        piece = x.astype(jnp.bfloat16).astype(jnp.float32)
+        pieces.append(piece)
+        x = x - piece
+    return pieces
+
+
+def stack16(x, parts):
+    pieces = split16(x, parts)
+    rows = x.shape[0] * parts
+    if rows % 16:
+        pieces.append(jnp.zeros((16 - rows % 16, x.shape[1]), jnp.float32))
+    return jnp.concatenate(pieces, axis=0).astype(jnp.bfloat16)
+
+
+def cross_parts(a, b):
+    return (
+        a[1:2] * b[2:3] - a[2:3] * b[1:2],
+        a[2:3] * b[0:1] - a[0:1] * b[2:3],
+        a[0:1] * b[1:2] - a[1:2] * b[0:1],
+    )
 
 
 def box_body(center_ref, rows_ref, basis_ref, block_ref, wave_ref, lanes_ref, parts_ref):
     b = pl.program_id(0)
     count = rows_ref.shape[0]
+    coef = basis_ref.shape[1]
     cx, cy, cz = center_ref[0, b], center_ref[1, b], center_ref[2, b]
     fx, fy, fz = basis_ref[0:1, :], basis_ref[1:2, :], basis_ref[2:3, :]
     phase = basis_ref[3:4, :]
-    ux, uy, uz = basis_ref[4:5, :], basis_ref[5:6, :], basis_ref[6:7, :]
+    lanes = jnp.concatenate(
+        [rows_ref[i * LANES : (i + 1) * LANES, :].T[:8] for i in range(count // LANES)], axis=1
+    )
+    lanes_ref[0] = lanes
+    zero = jnp.zeros((1, count), jnp.float32)
+    table = jnp.concatenate(
+        [lanes[3:6], zero, *cross_parts(lanes[3:6], lanes[0:3]), zero], axis=0
+    )
+    parts = stack16(table, 3)
+    parts_ref[0] = parts
     chunk = 32
-    total = jnp.zeros((8, fx.shape[1]), jnp.float32)
+    highs, lows = [], []
     for c in range(count // chunk):
         r = rows_ref[c * chunk : (c + 1) * chunk, :]
         turns = (
             fx * (r[:, 0:1] - cx) + fy * (r[:, 1:2] - cy) + fz * (r[:, 2:3] - cz) + phase
         )
         wave = cos_turns(turns)
-        wave_ref[c * chunk : (c + 1) * chunk, :] = wave
-        charge = ux * r[:, 3:4] + uy * r[:, 4:5] + uz * r[:, 5:6]
-        product = charge * wave
-        for s in range(chunk // 8):
-            total = total + product[s * 8 : (s + 1) * 8]
-    block_ref[0] = jnp.sum(total, axis=0, keepdims=True)
-    lanes = jnp.concatenate(
-        [rows_ref[i * LANES : (i + 1) * LANES, :].T[:8] for i in range(count // LANES)], axis=1
-    )
-    lanes_ref[0] = lanes
-    x, y, z = lanes[0:1], lanes[1:2], lanes[2:3]
-    sx, sy, sz = lanes[3:4], lanes[4:5], lanes[5:6]
-    zero = jnp.zeros_like(x)
-    table = jnp.concatenate(
-        [sx, sy, sz, zero, sy * z - sz * y, sz * x - sx * z, sx * y - sy * x, zero], axis=0
-    )
-    high = table.astype(jnp.bfloat16).astype(jnp.float32)
-    parts_ref[0] = jnp.concatenate([high, table - high], axis=0).astype(jnp.bfloat16)
+        high = wave.astype(jnp.bfloat16)
+        highs.append(high)
+        lows.append((wave - high.astype(jnp.float32)).astype(jnp.bfloat16))
+    high = jnp.concatenate(highs, axis=0)
+    low = jnp.concatenate(lows, axis=0)
+    wave_ref[:, :coef] = high
+    wave_ref[:, coef:] = low
+    sums = jnp.dot(parts, high, preferred_element_type=jnp.float32)
+    sums = sums + jnp.dot(parts, low, preferred_element_type=jnp.float32)
+    sums = sums[0:8] + sums[8:16] + sums[16:24]
+    block_ref[0] = (
+        basis_ref[4:5, :] * sums[0:1]
+        + basis_ref[5:6, :] * sums[1:2]
+        + basis_ref[6:7, :] * sums[2:3]
+    )
 
 
 def box_call(center, rows, basis, boxes, per_box):
@@ -254,9 +306,9 @@
         grid=(boxes,),
         out_shape=(
             jax.ShapeDtypeStruct((boxes, 1, coef), jnp.float32),
-            jax.ShapeDtypeStruct((boxes * per_box, coef), jnp.float32),
+            jax.ShapeDtypeStruct((boxes * per_box, 2 * coef), jnp.bfloat16),
             jax.ShapeDtypeStruct((boxes, 8, per_box), jnp.float32),
-            jax.ShapeDtypeStruct((boxes, 16, per_box), jnp.bfloat16),
+            jax.ShapeDtypeStruct((boxes, 32, per_box), jnp.bfloat16),
         ),
         in_specs=[
             pl.BlockSpec(memory_space=pltpu.SMEM),
@@ -265,62 +317,68 @@
         ],
         out_specs=(
             pl.BlockSpec((1, 1, coef), lambda b: (b, 0, 0)),
-            pl.BlockSpec((per_box, coef), lambda b: (b, 0)),
+            pl.BlockSpec((per_box, 2 * coef), lambda b: (b, 0)),
             pl.BlockSpec((1, 8, per_box), lambda b: (b, 0, 0)),
-            pl.BlockSpec((1, 16, per_box), lambda b: (b, 0, 0)),
+            pl.BlockSpec((1, 32, per_box), lambda b: (b, 0, 0)),
         ),
         compiler_params=pltpu.CompilerParams(vmem_limit_bytes=VMEM_LIMIT),
     )(center, rows, basis)
 
 
-def velocity_body(
-    near_ref, rows_ref, lanes_ref, parts_ref, wave_ref, exp_ref, dir_ref, out_ref, acc
-):
+def velocity_body(near_ref, rows_ref, lanes_ref, parts_ref, wave_ref, exp_ref, dir_ref, out_ref):
     b = pl.program_id(0)
     per_box = wave_ref.shape[0]
-    lanes = lanes_ref[b]
-    tx, ty, tz = lanes[0:1], lanes[1:2], lanes[2:3]
-    acc[...] = jnp.zeros_like(acc)
-    chunk = 64
-    for v in range(near_ref.shape[1]):
-        j = near_ref[b, v]
-
-        @pl.when(j >= 0)
-        def _():
-            start = j * per_box
-            pieces = []
-            for c in range(per_box // chunk):
-                at = pl.multiple_of(start + c * chunk, chunk)
-                s = rows_ref[pl.ds(at, chunk), :]
-                dx = tx - s[:, 0:1]
-                dy = ty - s[:, 1:2]
-                dz = tz - s[:, 2:3]
-                r = lax.rsqrt(dx * dx + dy * dy + dz * dz + core_square)
-                pieces.append((r * r * r).astype(jnp.bfloat16))
-            factor = jnp.concatenate(pieces, axis=0)
-            acc[...] += jnp.dot(parts_ref[j], factor, preferred_element_type=jnp.float32)
-
-    sums = acc[...]
-    sums = sums[0:8] + sums[8:16]
-    ax, ay, az = sums[0:1], sums[1:2], sums[2:3]
-    nx = ay * tz - az * ty - sums[4:5]
-    ny = az * tx - ax * tz - sums[5:6]
-    nz = ax * ty - ay * tx - sums[6:7]
-    near = jnp.concatenate([nx, ny, nz, jnp.zeros((5, per_box), jnp.float32)], axis=0)
-    near = near * inv_four_pi
-    high, low = split16(wave_ref[...] * exp_ref[0])
-    table = dir_ref[...]
-    both = jnp.dot(high, table, preferred_element_type=jnp.float32)
-    both = both + jnp.dot(low, table, preferred_element_type=jnp.float32)
-    far = both[:, :LANES] + both[:, LANES:]
-    for i in range(per_box // LANES):
-        out_ref[i * LANES : (i + 1) * LANES, :] = far[
-            i * LANES : (i + 1) * LANES
-        ] + lanes_to_rows(near[:, i * LANES : (i + 1) * LANES])
-
-
-def velocity_call(near, rows, lanes, parts, wave, exps, table, boxes, per_box):
-    coef = wave.shape[1]
+    coef = dir_ref.shape[1]
+    near_count = near_ref.shape[1]
+    chunk = 32
+
+    def pair_sums(j, target):
+        tx, ty, tz = target[0:1], target[1:2], target[2:3]
+        pieces = []
+        for c in range(per_box // chunk):
+            at = pl.multiple_of(j * per_box + c * chunk, chunk)
+            s = rows_ref[pl.ds(at, chunk), :]
+            dx = tx - s[:, 0:1]
+            dy = ty - s[:, 1:2]
+            dz = tz - s[:, 2:3]
+            r = lax.rsqrt(dx * dx + dy * dy + dz * dz + core_square)
+            pieces.append((r * r * r).astype(jnp.bfloat16))
+        factor = jnp.concatenate(pieces, axis=0)
+        return jnp.dot(parts_ref[j], factor, preferred_element_type=jnp.float32)
+
+    def whole_box(count):
+        target = lanes_ref[b]
+        table = stack16(dir_ref[...] * exp_ref[0], 2)
+        contract = (((1,), (1,)), ((), ()))
+        far = lax.dot_general(
+            table, wave_ref[:, :coef], contract, preferred_element_type=jnp.float32
+        )
+        far = far + lax.dot_general(
+            table, wave_ref[:, coef:], contract, preferred_element_type=jnp.float32
+        )
+        far = far[0:8] + far[8:16]
+        sums = pair_sums(near_ref[b, 0], target)
+        for v in range(1, count):
+            sums = sums + pair_sums(near_ref[b, v], target)
+        sums = sums[0:8] + sums[8:16] + sums[16:24]
+        near = jnp.concatenate(
+            [*cross_parts(sums[0:3], target[0:3]), jnp.zeros((5, per_box), jnp.float32)], axis=0
+        ) - jnp.concatenate([sums[4:7], jnp.zeros((5, per_box), jnp.float32)], axis=0)
+        total = near * inv_four_pi + far
+        for i in range(per_box // LANES):
+            out_ref[i * LANES : (i + 1) * LANES, :] = lanes_to_rows(
+                total[:, i * LANES : (i + 1) * LANES]
+            )
+
+    held = (near_ref[b, 0] >= 0).astype(jnp.int32)
+    for v in range(1, near_count):
+        held = held + (near_ref[b, v] >= 0).astype(jnp.int32)
+    for count in range(1, near_count + 1):
+        pl.when(held == count)(functools.partial(whole_box, count))
+
+
+def velocity_call(near, rows, lanes, parts, wave, exps, basis_dir, boxes, per_box):
+    coef = basis_dir.shape[1]
     return pl.pallas_call(
         velocity_body,
         grid=(boxes,),
@@ -330,19 +388,18 @@
             pl.BlockSpec(memory_space=pltpu.VMEM),
             pl.BlockSpec(memory_space=pltpu.VMEM),
             pl.BlockSpec(memory_space=pltpu.VMEM),
-            pl.BlockSpec((per_box, coef), lambda b: (b, 0)),
+            pl.BlockSpec((per_box, 2 * coef), lambda b: (b, 0)),
             pl.BlockSpec((1, 1, coef), lambda b: (b, 0, 0)),
             pl.BlockSpec(memory_space=pltpu.VMEM),
         ],
         out_specs=pl.BlockSpec((per_box, LANES), lambda b: (b, 0)),
-        scratch_shapes=[pltpu.VMEM((16, per_box), jnp.float32)],
         compiler_params=pltpu.CompilerParams(vmem_limit_bytes=VMEM_LIMIT),
-    )(near, rows, lanes, parts, wave, exps, table)
+    )(near, rows, lanes, parts, wave, exps, basis_dir)
 
 
 def per_device(
+    n_age,
     n_box,
-    groups,
     position,
     strength,
     node_box,
@@ -356,6 +413,7 @@
     basis_phase,
     translation,
 ):
+    groups = n_age * n_box
     node_count = position.shape[1]
     box_local = box_order.shape[0]
     slots_total = 2 * node_count
@@ -366,7 +424,7 @@
     box_total = groups * box_local
 
     padded_order = jnp.pad(box_order, (0, LANES - box_local)).reshape(1, LANES)
-    all_order = gather_blocks(padded_order, n_box, groups, 0)[:, 0, :box_local].reshape(-1)
+    all_order = gather_blocks(padded_order, n_age, n_box, 0)[:, :, 0, :box_local].reshape(-1)
 
     node_slot = jnp.sum(
         jnp.where(
@@ -421,15 +479,13 @@
     )
     sums, wave, lanes, parts = box_call(box_center, rows, basis, box_local, per_box)
     local_blocks = sums.reshape(box_local, coef).astype(jnp.bfloat16)
-    all_blocks = gather_blocks(local_blocks, n_box, groups, 1).reshape(box_total, coef)
+    all_blocks = gather_blocks(local_blocks, n_age, n_box, 1).reshape(box_total, coef)
     mixed = jnp.dot(list_counts, all_blocks, preferred_element_type=jnp.float32)
     mixed = mixed.astype(jnp.bfloat16).reshape(kind_count, box_local, coef)
     expansions = jnp.einsum(
         "tjc,tkc->jk", mixed, translation, preferred_element_type=jnp.float32
     )
-    dir_high, dir_low = split16(basis_dir.T)
-    pad = ((0, 0), (0, LANES - 3))
-    table = jnp.concatenate([jnp.pad(dir_high, pad), jnp.pad(dir_low, pad)], axis=1)
+    dir_rows = jnp.pad(basis_dir, ((0, 5), (0, 0)))
     vel_rows = velocity_call(
         near_local,
         rows,
@@ -437,7 +493,7 @@
         parts,
         wave,
         expansions.reshape(box_local, 1, coef),
-        table,
+        dir_rows,
         box_local,
         per_box,
     )
@@ -458,7 +514,7 @@
 
 def solution(mesh):
     n_box = mesh.shape["box"]
-    groups = mesh.shape["age"] * n_box
+    n_age = mesh.shape["age"]
     placed = (
         P(None, AXES),
         P(None, AXES),
@@ -474,7 +530,7 @@
         P(),
     )
     return jax.shard_map(
-        functools.partial(per_device, n_box, groups),
+        functools.partial(per_device, n_age, n_box),
         mesh=mesh,
         in_specs=placed,
         out_specs=P(None, AXES),

time: 194 us -> 157 us (0.81)
  Pallas kernels: 153 us -> 115 us
  blocking collectives: 10.1 us -> 12.4 us
    pallas_call x4, Pallas kernels: 59.8 us -> 40.4 us  [permute_call(): pl.pallas_call(body, out_shape=jax.ShapeDtypeStruct(out_shape, jnp.float3...]
    pallas_call x1, Pallas kernels: 45.8 us -> 30.5 us  [velocity_call(): pl.pallas_call(velocity_body, grid=(boxes,), out_shape=jax.ShapeDtypeStru...]
    pallas_call x2, Pallas kernels: 29.1 us -> 25.9 us  [gather_blocks(): pl.pallas_call(functools.partial(gather_body, n_age, n_box), out_shape=ja...]
    all_to_all x1, blocking collectives: 10.1 us -> 12.4 us  [per_device(): lax.all_to_all(back[:3], AXES, split_axis=1, concat_axis=1, tiled=True)]
where the time goes in v1:
time: 157 us
  Pallas kernels  115 us (73%)
  blocking collectives  12.4 us (8%)
  local copies, waits for them, and re-layouts  7.3 us (5%)
  other arithmetic  6.52 us (4%)
  matrix products  6.39 us (4%)
  waiting for transfers between devices  5.19 us (3%)
  starting transfers between devices  3.62 us (2%)
    pallas_call x4, Pallas kernels, permute_call(): pl.pallas_call(body, out_shape=jax.ShapeDtypeStruct(out_shape, jnp.float3...  40.4 us
    pallas_call x1, Pallas kernels, velocity_call(): pl.pallas_call(velocity_body, grid=(boxes,), out_shape=jax.ShapeDtypeStru...  30.5 us
    pallas_call x2, Pallas kernels, gather_blocks(): pl.pallas_call(functools.partial(gather_body, n_age, n_box), out_shape=ja...  25.9 us
    pallas_call x1, Pallas kernels, box_call(): pl.pallas_call(box_body, grid=(boxes,), out_shape=(jax.ShapeDtypeStruct((...  18.4 us
    all_to_all x1, blocking collectives, per_device(): lax.all_to_all(back[:3], AXES, split_axis=1, concat_axis=1, tiled=True)  12.4 us
    all_to_all x1, waiting for transfers between devices, per_device(): got = lax.all_to_all(payload, AXES, split_axis=1, concat_axis=1, tiled=True)  5.19 us
    all_to_all x1, starting transfers between devices, per_device(): got = lax.all_to_all(payload, AXES, split_axis=1, concat_axis=1, tiled=True)  3.62 us
  transfers between devices with their start and end apart: 1, of which 1 were waited for; matrix products, arithmetic and copies ran while one was open for 3% of the time, Pallas kernels for 0%

profile of v1, /device:TPU:0, one launch (start us, length us, event | category | flops | bytes accessed | tf_op | source)
XLA Modules:
  0.0 156.8 jit_solution(5219702958153851625)
XLA Ops:
  0.0 1.3 pad_bitcast_fusion.x_ref
  1.3 12.6 %shard_map.154 = s32[8,4,1,128]{3,2,1,0:T(1,128)} custom-call(s32[1,128]{1,0:T(1,128)} %pad_bitcast_fusion.x_ref), custom_call_target="tpu_custom_call" | custom-call | tf_op jit(solution)/shard_map/pallas_call | solution.py:106
  14.0 0.8 slice_reduce_fusion
  14.8 3.0 %select_reduce_fusion = s32[4096]{0:T(1024)S(1)} fusion(s32[4096]{0:T(1024)} %param.18, s32[1024]{0:T(1024)S(1)} %eq.87), kind=kLoop, calls=%fused_computation | loop fusion | flops 12578816 | bytes 36864 | tf_op jit(solution)/shard_map/reduce_sum | solution.py:429
  17.9 0.2 convert_reduce_fusion.1
  18.1 0.8 fusion.35
  18.9 1.0 fusion.13
  20.1 0.9 maximum_maximum_fusion.x_ref
  21.1 8.9 %shard_map.155 = f32[8,8192]{1,0:T(8,128)} custom-call(s32[4096]{0:T(1024)S(1)} %fusion.21.idx_ref, f32[8,4096]{1,0:T(8,128)S(1)} %maximum_maximum_fusion.x_ref), custom_call_target="tpu_custom_call" | custom-call | tf_op jit(solution)/shard_map/pallas_call | solution.py:199
  30.0 3.6 %all-to-all-start = ((f32[8,32,256]{2,0,1:T(8,128)}), f32[8,32,256]{2,0,1:T(8,128)S(1)}, u32[]{:S(2)}, u32[]{:S(2)}) async-start(f32[8,32,256]{2,0,1:T(8,128)} %bitcast.5), calls=%async_computation | async-start | bytes 524288 | tf_op jit(solution)/shard_map/all_to_all | solution.py:446
  33.6 0.7 broadcast_multiply_fusion.2
  34.3 0.7 broadcast_multiply_fusion.1
  35.0 1.6 %fusion.7 = bf16[16,32,1024]{2,0,1:T(8,128)(2,1)S(1)} fusion(s32[1024]{0:T(1024)S(1)} %eq.87, s32[32,32]{1,0:T(8,128)} %param.22, s32[32,32]{1,0:T(8,128)} %param.23), kind=kOutput, calls=%fused_computation.6 | convolution fusion | flops 35143680 | bytes 1060864 | tf_op jit(solution)/shard_map/jlt,jlb->tjb/dot_general | solution.py:452
  36.6 0.2 select_reduce_fusion.1
  36.9 1.6 %copy.33 = bf16[16,32,1024]{2,1,0:T(8,128)(2,1)} copy(bf16[16,32,1024]{2,0,1:T(8,128)(2,1)S(1)} %fusion.7) | data formatting | bytes 2097152 | tf_op jit(solution)/shard_map/convert_element_type | solution.py:455
  38.6 5.2 %all-to-all-done = f32[8,32,256]{2,0,1:T(8,128)S(1)} async-done(((f32[8,32,256]{2,0,1:T(8,128)}), f32[8,32,256]{2,0,1:T(8,128)S(1)}, u32[]{:S(2)}, u32[]{:S(2)}) %all-to-all-start) | async-done | bytes 262176 | tf_op jit(solution)/shard_map/all_to_all | solution.py:446
  43.8 0.1 compare_reduce_fusion
  44.0 0.4 convert_reduce_fusion
  44.3 0.1 fusion.34
  44.5 0.4 fusion.11
  44.8 12.1 %shard_map.156.rows_ref = f32[8200,128]{1,0:T(8,128)S(1)} custom-call(s32[8192]{0:T(1024)S(1)} %get-tuple-element.14.idx_ref, f32[8,8192]{1,0:T(8,128)S(1)} %bitcast.56), custom_call_target="tpu_custom_call" | custom-call | tf_op jit(solution)/shard_map/pallas_call | solution.py:199
  56.9 18.4 %shard_map.157 = (f32[32,1,256]{2,1,0:T(1,128)S(1)}, bf16[8192,512]{1,0:T(8,128)(2,1)}, f32[32,8,256]{2,1,0:T(8,128)S(1)}, bf16[32,32,256]{2,1,0:T(8,128)(2,1)S(1)}) custom-call(f32[3,32]{1,0:T(4,128)S(1)} %copy-done.2, f32[8200,128]{1,0:T(8,128)S(1)} %shard_map.156.rows_ref, f32[8,256]{1,0:T(8,128)S(1)} %get-tuple-element.18.basis_ref), custom_call_target="tpu_custom_call" | custom-call | tf_op jit(solution)/shard_map/pallas_call | solution.py:304
  75.4 2.0 %copy-done.1 = f32[8200,128]{1,0:T(8,128)} copy-done((f32[8200,128]{1,0:T(8,128)}, f32[8200,128]{1,0:T(8,128)S(1)}, u32[]{:S(2)}) %copy-start.1) | copy-done | bytes 4198424
  77.3 0.6 copy.39
  77.9 13.3 %shard_map.158 = bf16[8,4,32,256]{3,2,1,0:T(8,128)(2,1)} custom-call(bf16[32,256]{1,0:T(8,128)(2,1)} %bitcast.66), custom_call_target="tpu_custom_call" | custom-call | tf_op jit(solution)/shard_map/pallas_call | solution.py:106
  91.2 1.8 %convolution_convert_fusion = bf16[512,256]{1,0:T(8,128)(2,1)S(1)} fusion(bf16[512,1024]{1,0:T(8,128)(2,1)} %bitcast.57, bf16[1024,256]{1,0:T(8,128)(2,1)} %bitcast.58), kind=kOutput, calls=%fused_computation.12 | convolution fusion | flops 268566528 | bytes 1835008 | tf_op jit(solution)/shard_map/dot_general | solution.py:483
  93.0 0.7 convolution_bitcast_fusion
  93.8 30.5 %shard_map.159.x_ref = f32[8192,128]{1,0:T(8,128)S(1)} custom-call(s32[32,4]{1,0:T(8,128)S(1)} %broadcast_add_fusion.near_ref, f32[8200,128]{1,0:T(8,128)} %copy-done.1, f32[32,8,256]{2,1,0:T(8,128)S(1)} %get-tuple-element.9.lanes_ref, bf16[32,32,256]{2,1,0:T(8,128)(2,1)S(1)} %get-tuple-element.10.parts_ref, bf16[8192,512]{1,0:T(8,128)(2,1)} %get-tuple-element.11.wave_ref, ...), custom_call_target="tpu_custom_call" | custom-call | tf_op jit(solution)/shard_map/pallas_call | solution.py:382
  124.3 11.6 %shard_map.160 = f32[8,8192]{1,0:T(8,128)S(1)} custom-call(s32[8192]{0:T(1024)S(1)} %get-tuple-element.13.idx_ref, f32[8192,128]{1,0:T(8,128)S(1)} %shard_map.159.x_ref), custom_call_target="tpu_custom_call" | custom-call | tf_op jit(solution)/shard_map/pallas_call | solution.py:199
  135.9 12.4 %all_to_all.23 = f32[3,32,256]{2,0,1:T(4,128)S(1)} all-to-all(f32[3,32,256]{2,0,1:T(4,128)S(1)} %bitcast.60), channel_id=1, replica_groups=mesh['age'=8,'box'=4] {'age','box'}, dimensions={1} | all-to-all | bytes 196608 | tf_op jit(solution)/shard_map/all_to_all | solution.py:507
  148.3 7.8 %shard_map.161 = f32[8,4096]{1,0:T(8,128)S(1)} custom-call(s32[4096]{0:T(1024)S(1)} %fusion.21.idx_ref, f32[8,8192]{1,0:T(8,128)S(1)} %pad.14.x_ref), custom_call_target="tpu_custom_call" | custom-call | tf_op jit(solution)/shard_map/pallas_call | solution.py:199
  156.1 0.6 slice.19
  (30 shorter events, 0.7 us)
Async XLA Ops:
  0.0 93.0 %copy-start = (bf16[16,256,256]{2,1,0:T(8,128)(2,1)S(1)}, bf16[16,256,256]{2,1,0:T(8,128)(2,1)}, u32[]{:S(2)}) copy-start(bf16[16,256,256]{2,1,0:T(8,128)(2,1)} %param.27) | copy-start | bytes 6291460
  0.0 44.5 %copy-start.7 = (bf16[128,128,1]{1,0,2:T(8,128)(2,1)S(1)}, bf16[128,128,1]{1,0,2:T(8,128)(2,1)}, u32[]{:S(2)}) copy-start(bf16[128,128,1]{1,0,2:T(8,128)(2,1)} %constant.56) | copy-start | bytes 98308
  0.0 44.3 %copy-start.3 = (bf16[64,64]{1,0:T(8,128)(2,1)S(1)}, bf16[64,64]{1,0:T(8,128)(2,1)}, u32[]{:S(2)}) copy-start(bf16[64,64]{1,0:T(8,128)(2,1)} %constant.49.clone) | copy-start | bytes 24580
  0.0 36.6 %copy-start.6 = (s32[32]{0:T(128)S(1)}, s32[32]{0:T(128)}, u32[]{:S(2)}) copy-start(s32[32]{0:T(128)} %param.19) | copy-start | bytes 388
  0.0 36.6 %copy-start.5 = (s32[32,4]{0,1:T(4,128)S(1)}, s32[32,4]{0,1:T(4,128)}, u32[]{:S(2)}) copy-start(s32[32,4]{0,1:T(4,128)} %param.21) | copy-start | bytes 1540
  0.0 38.5 %copy-start.4 = (f32[3,256]{1,0:T(4,128)S(1)}, f32[3,256]{1,0:T(4,128)}, u32[]{:S(2)}) copy-start(f32[3,256]{1,0:T(4,128)} %param.24) | copy-start | bytes 9220
  30.0 13.8 %all-to-all-start = ((f32[8,32,256]{2,0,1:T(8,128)}), f32[8,32,256]{2,0,1:T(8,128)S(1)}, u32[]{:S(2)}, u32[]{:S(2)}) async-start(f32[8,32,256]{2,0,1:T(8,128)} %bitcast.5), calls=%async_computation | async-start | bytes 524288 | tf_op jit(solution)/shard_map/all_to_all | solution.py:446
  36.9 20.0 %copy-start.2 = (f32[3,32]{1,0:T(4,128)S(1)}, f32[3,32]{1,0:T(4,128)}, u32[]{:S(2)}) copy-start(f32[3,32]{1,0:T(4,128)} %center_ref.1) | copy-start | bytes 1156
  75.4 2.0 %copy-start.1 = (f32[8200,128]{1,0:T(8,128)}, f32[8200,128]{1,0:T(8,128)S(1)}, u32[]{:S(2)}) copy-start(f32[8200,128]{1,0:T(8,128)S(1)} %shard_map.156.rows_ref) | copy-start | bytes 12595204

commit v2 on v1

--- a/solution.py
+++ b/solution.py
@@ -13,7 +13,7 @@
 inv_four_pi = 0.07957747154594767
 inv_two_pi = 0.15915494309189535
 LANES = 128
-VMEM_LIMIT = 48 * 1024 * 1024
+VMEM_LIMIT = 32 * 1024 * 1024
 
 
 def cos_coefficients(degree):
@@ -178,17 +178,6 @@
     take_lanes(placed, out_ref, out_ref.shape[1])
 
 
-def group_body(idx_ref, x_ref, out_ref, rows):
-    fill_rows(x_ref, rows, x_ref.shape[1])
-    zero_rows(out_ref)
-    scatter_rows(idx_ref, rows, out_ref, x_ref.shape[1])
-
-
-def ungroup_body(idx_ref, x_ref, out_ref, rows):
-    gather_rows(idx_ref, x_ref, rows, out_ref.shape[1])
-    take_lanes(rows, out_ref, out_ref.shape[1])
-
-
 def collect_body(idx_ref, x_ref, out_ref, src, rows):
     fill_rows(x_ref, src, x_ref.shape[1])
     gather_rows(idx_ref, src, rows, out_ref.shape[1])
@@ -257,77 +246,103 @@
     )
 
 
-def box_body(center_ref, rows_ref, basis_ref, block_ref, wave_ref, lanes_ref, parts_ref):
-    b = pl.program_id(0)
-    count = rows_ref.shape[0]
+def one_box(b, center_ref, basis_ref, freq_ref, rows_ref, block_ref, wave_ref, lanes_ref, parts_ref):
+    count = lanes_ref.shape[2]
+    at = pl.multiple_of(b * count, count)
     coef = basis_ref.shape[1]
     cx, cy, cz = center_ref[0, b], center_ref[1, b], center_ref[2, b]
-    fx, fy, fz = basis_ref[0:1, :], basis_ref[1:2, :], basis_ref[2:3, :]
-    phase = basis_ref[3:4, :]
     lanes = jnp.concatenate(
-        [rows_ref[i * LANES : (i + 1) * LANES, :].T[:8] for i in range(count // LANES)], axis=1
-    )
-    lanes_ref[0] = lanes
+        [rows_ref[pl.ds(at + i * LANES, LANES), :].T[:8] for i in range(count // LANES)], axis=1
+    )
+    lanes_ref[b] = lanes
     zero = jnp.zeros((1, count), jnp.float32)
     table = jnp.concatenate(
         [lanes[3:6], zero, *cross_parts(lanes[3:6], lanes[0:3]), zero], axis=0
     )
     parts = stack16(table, 3)
-    parts_ref[0] = parts
+    parts_ref[b] = parts
+    one = jnp.ones((1, count), jnp.float32)
+    offset = jnp.concatenate(
+        [lanes[0:1] - cx, lanes[1:2] - cy, lanes[2:3] - cz, one, jnp.zeros((4, count), jnp.float32)],
+        axis=0,
+    )
+    o1, o2, o3 = split16(offset, 3)
+    stacked = jnp.concatenate([o3, o2, o2, o1, o1, o1], axis=0).astype(jnp.bfloat16)
+    turns = lax.dot_general(
+        stacked, freq_ref[...], (((0,), (0,)), ((), ())), preferred_element_type=jnp.float32
+    )
     chunk = 32
     highs, lows = [], []
     for c in range(count // chunk):
-        r = rows_ref[c * chunk : (c + 1) * chunk, :]
-        turns = (
-            fx * (r[:, 0:1] - cx) + fy * (r[:, 1:2] - cy) + fz * (r[:, 2:3] - cz) + phase
-        )
-        wave = cos_turns(turns)
+        wave = cos_turns(turns[c * chunk : (c + 1) * chunk])
         high = wave.astype(jnp.bfloat16)
         highs.append(high)
         lows.append((wave - high.astype(jnp.float32)).astype(jnp.bfloat16))
     high = jnp.concatenate(highs, axis=0)
     low = jnp.concatenate(lows, axis=0)
-    wave_ref[:, :coef] = high
-    wave_ref[:, coef:] = low
+    wave_ref[pl.ds(at, count), :coef] = high
+    wave_ref[pl.ds(at, count), coef:] = low
     sums = jnp.dot(parts, high, preferred_element_type=jnp.float32)
     sums = sums + jnp.dot(parts, low, preferred_element_type=jnp.float32)
     sums = sums[0:8] + sums[8:16] + sums[16:24]
-    block_ref[0] = (
-        basis_ref[4:5, :] * sums[0:1]
-        + basis_ref[5:6, :] * sums[1:2]
-        + basis_ref[6:7, :] * sums[2:3]
-    )
-
-
-def box_call(center, rows, basis, boxes, per_box):
+    block_ref[b] = (
+        basis_ref[0:1, :] * sums[0:1]
+        + basis_ref[1:2, :] * sums[1:2]
+        + basis_ref[2:3, :] * sums[2:3]
+    )
+
+
+def group_body(
+    idx_ref, center_ref, x_ref, basis_ref, freq_ref,
+    rows_ref, block_ref, wave_ref, lanes_ref, parts_ref, scattered,
+):
+    fill_rows(x_ref, scattered, x_ref.shape[1])
+    zero_rows(rows_ref)
+    scatter_rows(idx_ref, scattered, rows_ref, x_ref.shape[1])
+
+    def step(b, carry):
+        one_box(
+            b, center_ref, basis_ref, freq_ref, rows_ref, block_ref, wave_ref, lanes_ref, parts_ref
+        )
+        return carry
+
+    lax.fori_loop(0, block_ref.shape[0], step, 0, unroll=2)
+
+
+def split_body(x_ref, out_ref):
+    f1, f2, f3 = split16(x_ref[...], 3)
+    out_ref[...] = jnp.concatenate([f1, f2, f1, f3, f2, f1], axis=0).astype(jnp.bfloat16)
+
+
+def split_call(x):
+    return pl.pallas_call(
+        split_body, out_shape=jax.ShapeDtypeStruct((6 * x.shape[0], x.shape[1]), jnp.bfloat16)
+    )(x)
+
+
+def group_call(idx, center, got, basis, freq, boxes, per_box):
     coef = basis.shape[1]
+    slots = boxes * per_box
     return pl.pallas_call(
-        box_body,
-        grid=(boxes,),
+        group_body,
         out_shape=(
+            jax.ShapeDtypeStruct((slots + 8, LANES), jnp.float32),
             jax.ShapeDtypeStruct((boxes, 1, coef), jnp.float32),
-            jax.ShapeDtypeStruct((boxes * per_box, 2 * coef), jnp.bfloat16),
+            jax.ShapeDtypeStruct((slots, 2 * coef), jnp.bfloat16),
             jax.ShapeDtypeStruct((boxes, 8, per_box), jnp.float32),
             jax.ShapeDtypeStruct((boxes, 32, per_box), jnp.bfloat16),
         ),
-        in_specs=[
-            pl.BlockSpec(memory_space=pltpu.SMEM),
-            pl.BlockSpec((per_box, LANES), lambda b: (b, 0)),
-            pl.BlockSpec((8, coef), lambda b: (0, 0)),
-        ],
-        out_specs=(
-            pl.BlockSpec((1, 1, coef), lambda b: (b, 0, 0)),
-            pl.BlockSpec((per_box, 2 * coef), lambda b: (b, 0)),
-            pl.BlockSpec((1, 8, per_box), lambda b: (b, 0, 0)),
-            pl.BlockSpec((1, 32, per_box), lambda b: (b, 0, 0)),
-        ),
+        in_specs=[pl.BlockSpec(memory_space=pltpu.SMEM)] * 2
+        + [pl.BlockSpec(memory_space=pltpu.VMEM)] * 3,
+        out_specs=(pl.BlockSpec(memory_space=pltpu.VMEM),) * 5,
+        scratch_shapes=[pltpu.VMEM((slots, LANES), jnp.float32)],
         compiler_params=pltpu.CompilerParams(vmem_limit_bytes=VMEM_LIMIT),
-    )(center, rows, basis)
-
-
-def velocity_body(near_ref, rows_ref, lanes_ref, parts_ref, wave_ref, exp_ref, dir_ref, out_ref):
-    b = pl.program_id(0)
-    per_box = wave_ref.shape[0]
+    )(idx, center, got, basis, freq)
+
+
+def one_velocity(b, near_ref, rows_ref, lanes_ref, parts_ref, wave_ref, exp_ref, dir_ref, out_ref):
+    per_box = lanes_ref.shape[2]
+    here = pl.multiple_of(b * per_box, per_box)
     coef = dir_ref.shape[1]
     near_count = near_ref.shape[1]
     chunk = 32
@@ -348,13 +363,13 @@
 
     def whole_box(count):
         target = lanes_ref[b]
-        table = stack16(dir_ref[...] * exp_ref[0], 2)
+        table = stack16(dir_ref[...] * exp_ref[b], 2)
         contract = (((1,), (1,)), ((), ()))
         far = lax.dot_general(
-            table, wave_ref[:, :coef], contract, preferred_element_type=jnp.float32
+            table, wave_ref[pl.ds(here, per_box), :coef], contract, preferred_element_type=jnp.float32
         )
         far = far + lax.dot_general(
-            table, wave_ref[:, coef:], contract, preferred_element_type=jnp.float32
+            table, wave_ref[pl.ds(here, per_box), coef:], contract, preferred_element_type=jnp.float32
         )
         far = far[0:8] + far[8:16]
         sums = pair_sums(near_ref[b, 0], target)
@@ -366,7 +381,7 @@
         ) - jnp.concatenate([sums[4:7], jnp.zeros((5, per_box), jnp.float32)], axis=0)
         total = near * inv_four_pi + far
         for i in range(per_box // LANES):
-            out_ref[i * LANES : (i + 1) * LANES, :] = lanes_to_rows(
+            out_ref[pl.ds(here + i * LANES, LANES), :] = lanes_to_rows(
                 total[:, i * LANES : (i + 1) * LANES]
             )
 
@@ -377,24 +392,32 @@
         pl.when(held == count)(functools.partial(whole_box, count))
 
 
-def velocity_call(near, rows, lanes, parts, wave, exps, basis_dir, boxes, per_box):
-    coef = basis_dir.shape[1]
+def velocity_body(
+    idx_ref, near_ref, rows_ref, lanes_ref, parts_ref, wave_ref, exp_ref, dir_ref,
+    out_ref, vel, rows,
+):
+    def step(b, carry):
+        one_velocity(
+            b, near_ref, rows_ref, lanes_ref, parts_ref, wave_ref, exp_ref, dir_ref, vel
+        )
+        return carry
+
+    lax.fori_loop(0, lanes_ref.shape[0], step, 0)
+    gather_rows(idx_ref, vel, rows, out_ref.shape[1])
+    take_lanes(rows, out_ref, out_ref.shape[1])
+
+
+def velocity_call(idx, near, rows, lanes, parts, wave, exps, basis_dir):
+    slots = wave.shape[0]
     return pl.pallas_call(
         velocity_body,
-        grid=(boxes,),
-        out_shape=jax.ShapeDtypeStruct((boxes * per_box, LANES), jnp.float32),
-        in_specs=[
-            pl.BlockSpec(memory_space=pltpu.SMEM),
-            pl.BlockSpec(memory_space=pltpu.VMEM),
-            pl.BlockSpec(memory_space=pltpu.VMEM),
-            pl.BlockSpec(memory_space=pltpu.VMEM),
-            pl.BlockSpec((per_box, 2 * coef), lambda b: (b, 0)),
-            pl.BlockSpec((1, 1, coef), lambda b: (b, 0, 0)),
-            pl.BlockSpec(memory_space=pltpu.VMEM),
-        ],
-        out_specs=pl.BlockSpec((per_box, LANES), lambda b: (b, 0)),
+        out_shape=jax.ShapeDtypeStruct((8, slots), jnp.float32),
+        in_specs=[pl.BlockSpec(memory_space=pltpu.SMEM)] * 2
+        + [pl.BlockSpec(memory_space=pltpu.VMEM)] * 6,
+        out_specs=pl.BlockSpec(memory_space=pltpu.VMEM),
+        scratch_shapes=[pltpu.VMEM((slots, LANES), jnp.float32)] * 2,
         compiler_params=pltpu.CompilerParams(vmem_limit_bytes=VMEM_LIMIT),
-    )(near, rows, lanes, parts, wave, exps, basis_dir)
+    )(idx, near, rows, lanes, parts, wave, exps, basis_dir)
 
 
 def per_device(
@@ -467,17 +490,12 @@
     tile_at = jnp.where(
         live, got_label * per_box + ranks(got_label, box_local), slots_total
     )
-    rows = permute_call(group_body, tile_at, got, (slots_total + 8, LANES), (slots_total,))
-    basis = jnp.concatenate(
-        [
-            basis_freq * inv_two_pi,
-            basis_phase[None, :] * inv_two_pi,
-            basis_dir,
-            jnp.zeros((1, coef), jnp.float32),
-        ],
-        axis=0,
-    )
-    sums, wave, lanes, parts = box_call(box_center, rows, basis, box_local, per_box)
+    dir_rows = jnp.pad(basis_dir, ((0, 5), (0, 0)))
+    waves = jnp.concatenate([basis_freq, basis_phase[None, :]], axis=0) * inv_two_pi
+    freq = split_call(jnp.pad(waves, ((0, 4), (0, 0))))
+    rows, sums, wave, lanes, parts = group_call(
+        tile_at, box_center, got, dir_rows, freq, box_local, per_box
+    )
     local_blocks = sums.reshape(box_local, coef).astype(jnp.bfloat16)
     all_blocks = gather_blocks(local_blocks, n_age, n_box, 1).reshape(box_total, coef)
     mixed = jnp.dot(list_counts, all_blocks, preferred_element_type=jnp.float32)
@@ -485,8 +503,8 @@
     expansions = jnp.einsum(
         "tjc,tkc->jk", mixed, translation, preferred_element_type=jnp.float32
     )
-    dir_rows = jnp.pad(basis_dir, ((0, 5), (0, 0)))
-    vel_rows = velocity_call(
+    back = velocity_call(
+        jnp.minimum(tile_at, slots_total - 1),
         near_local,
         rows,
         lanes,
@@ -494,15 +512,6 @@
         wave,
         expansions.reshape(box_local, 1, coef),
         dir_rows,
-        box_local,
-        per_box,
-    )
-    back = permute_call(
-        ungroup_body,
-        jnp.minimum(tile_at, slots_total - 1),
-        vel_rows,
-        (8, slots_total),
-        (slots_total,),
     )
     returned = lax.all_to_all(back[:3], AXES, split_axis=1, concat_axis=1, tiled=True)
     returned = jnp.pad(returned, ((0, 5), (0, 0)))

time: 157 us -> 152 us (0.968)
  Pallas kernels: 115 us -> 104 us
  local copies, waits for them, and re-layouts: 7.3 us -> 15.2 us
  waiting for transfers between devices: 5.19 us -> 2.64 us
    pallas_call x4 -> x2, Pallas kernels: 40.4 us -> 16.7 us  [permute_call(): pl.pallas_call(body, out_shape=jax.ShapeDtypeStruct(out_shape, jnp.float3...]
    pallas_call x2 -> x3, Pallas kernels: 48.9 us -> 61.5 us  [the longest x1 35.4 us: velocity_call(): pl.pallas_call(velocity_body, out_shape=jax.ShapeDtypeStruct((8, slots),...]
    unnamed x16 -> x18, local copies, waits for them, and re-layouts: 2 us -> 8.59 us
    all_to_all x1, waiting for transfers between devices: 5.19 us -> 2.64 us  [per_device(): got = lax.all_to_all(payload, AXES, split_axis=1, concat_axis=1, tiled=True)]
  transfers between devices with their start and end apart: 1 -> 1, of which waited for: 1 -> 1; matrix products, arithmetic and copies ran while one was open for 3% -> 4% of each run, Pallas kernels for 0% -> 1%
where the time goes in v2:
time: 152 us; the launch traced here: 151 us
  Pallas kernels  104 us (68%)
  local copies, waits for them, and re-layouts  15.2 us (10%)
  blocking collectives  12 us (8%)
  matrix products  6.56 us (4%)
  other arithmetic  6.49 us (4%)
  starting transfers between devices  3.62 us (2%)
  waiting for transfers between devices  2.64 us (2%)
    pallas_call x1, Pallas kernels, velocity_call(): pl.pallas_call(velocity_body, out_shape=jax.ShapeDtypeStruct((8, slots),...  35.4 us
    pallas_call x2, Pallas kernels, gather_blocks(): pl.pallas_call(functools.partial(gather_body, n_age, n_box), out_shape=ja...  25.9 us
    pallas_call x1, Pallas kernels, group_call(): pl.pallas_call(group_body, out_shape=(jax.ShapeDtypeStruct((slots + 8, LA...  24.8 us
    pallas_call x2, Pallas kernels, permute_call(): pl.pallas_call(body, out_shape=jax.ShapeDtypeStruct(out_shape, jnp.float3...  16.7 us
    all_to_all x1, blocking collectives, per_device(): lax.all_to_all(back[:3], AXES, split_axis=1, concat_axis=1, tiled=True)  12 us
    unnamed x18, local copies, waits for them, and re-layouts  8.59 us
    all_to_all x1, starting transfers between devices, per_device(): got = lax.all_to_all(payload, AXES, split_axis=1, concat_axis=1, tiled=True)  3.62 us
  transfers between devices with their start and end apart: 1, of which 1 were waited for; matrix products, arithmetic and copies ran while one was open for 4% of the time, Pallas kernels for 1%

profile of v2, /device:TPU:0, one launch (start us, length us, event | category | flops | bytes accessed | tf_op | source)
XLA Modules:
  0.0 150.8 jit_solution(2679259121507448637)
XLA Ops:
  0.0 1.3 pad_bitcast_fusion.x_ref
  1.3 12.6 %shard_map.154 = s32[8,4,1,128]{3,2,1,0:T(1,128)} custom-call(s32[1,128]{1,0:T(1,128)} %pad_bitcast_fusion.x_ref), custom_call_target="tpu_custom_call" | custom-call | tf_op jit(solution)/shard_map/pallas_call | solution.py:106
  14.0 0.8 slice_reduce_fusion
  14.8 3.0 %select_reduce_fusion = s32[4096]{0:T(1024)S(1)} fusion(s32[4096]{0:T(1024)} %param.18, s32[1024]{0:T(1024)S(1)} %eq.87), kind=kLoop, calls=%fused_computation | loop fusion | flops 12578816 | bytes 36864 | tf_op jit(solution)/shard_map/reduce_sum | solution.py:452
  17.9 0.2 convert_reduce_fusion.1
  18.1 0.8 fusion.34
  18.9 1.0 fusion.13
  20.1 0.9 maximum_maximum_fusion.x_ref
  21.1 8.9 %shard_map.155 = f32[8,8192]{1,0:T(8,128)} custom-call(s32[4096]{0:T(1024)S(1)} %fusion.21.idx_ref, f32[8,4096]{1,0:T(8,128)S(1)} %maximum_maximum_fusion.x_ref), custom_call_target="tpu_custom_call" | custom-call | tf_op jit(solution)/shard_map/pallas_call | solution.py:188
  30.0 3.6 %all-to-all-start = ((f32[8,32,256]{2,0,1:T(8,128)}), f32[8,32,256]{2,0,1:T(8,128)S(1)}, u32[]{:S(2)}, u32[]{:S(2)}) async-start(f32[8,32,256]{2,0,1:T(8,128)} %bitcast.5), calls=%async_computation | async-start | bytes 524288 | tf_op jit(solution)/shard_map/all_to_all | solution.py:469
  33.6 0.9 select_reduce_fusion.1
  34.5 0.7 maximum_multiply_fusion
  35.2 0.6 pad.18.x_ref
  35.8 0.7 pad.17.basis_ref.dir_ref
  36.6 1.3 shard_map.156.freq_ref
  37.9 1.6 %fusion.7 = bf16[16,32,1024]{2,0,1:T(8,128)(2,1)S(1)} fusion(s32[1024]{0:T(1024)S(1)} %eq.87, s32[32,32]{1,0:T(8,128)} %param.22, s32[32,32]{1,0:T(8,128)} %param.23), kind=kOutput, calls=%fused_computation.6 | convolution fusion | flops 35143680 | bytes 1060864 | tf_op jit(solution)/shard_map/jlt,jlb->tjb/dot_general | solution.py:475
  39.5 1.6 %copy.33 = bf16[16,32,1024]{2,1,0:T(8,128)(2,1)} copy(bf16[16,32,1024]{2,0,1:T(8,128)(2,1)S(1)} %fusion.7) | data formatting | bytes 2097152 | tf_op jit(solution)/shard_map/convert_element_type | solution.py:478
  41.1 2.6 %all-to-all-done = f32[8,32,256]{2,0,1:T(8,128)S(1)} async-done(((f32[8,32,256]{2,0,1:T(8,128)}), f32[8,32,256]{2,0,1:T(8,128)S(1)}, u32[]{:S(2)}, u32[]{:S(2)}) %all-to-all-start) | async-done | bytes 262176 | tf_op jit(solution)/shard_map/all_to_all | solution.py:469
  44.0 0.4 convert_reduce_fusion
  44.5 0.4 fusion.11
  44.9 24.8 %shard_map.157 = (f32[8200,128]{1,0:T(8,128)S(1)}, f32[32,1,256]{2,1,0:T(1,128)S(1)}, bf16[8192,512]{1,0:T(8,128)(2,1)S(1)}, f32[32,8,256]{2,1,0:T(8,128)S(1)}, bf16[32,32,256]{2,1,0:T(8,128)(2,1)S(1)}) custom-call(s32[8192]{0:T(1024)S(1)} %get-tuple-element.16.idx_ref, f32[3,32]{1,0:T(4,128)S(1)} %copy-done.6, f32[8,8192]{1,0:T(8,128)S(1)} %bitcast.55, ...), custom_call_target="tpu_custom_call" | custom-call | tf_op jit(solution)/shard_map/pallas_call | solution.py:326
  69.7 3.2 %copy-done.1 = bf16[8192,512]{1,0:T(8,128)(2,1)} copy-done((bf16[8192,512]{1,0:T(8,128)(2,1)}, bf16[8192,512]{1,0:T(8,128)(2,1)S(1)}, u32[]{:S(2)}) %copy-start.1) | copy-done | bytes 8388632
  72.9 2.0 %copy-done.3 = f32[8200,128]{1,0:T(8,128)} copy-done((f32[8200,128]{1,0:T(8,128)}, f32[8200,128]{1,0:T(8,128)S(1)}, u32[]{:S(2)}) %copy-start.3) | copy-done | bytes 4198424
  74.9 0.6 copy.39
  75.5 13.3 %shard_map.158 = bf16[8,4,32,256]{3,2,1,0:T(8,128)(2,1)} custom-call(bf16[32,256]{1,0:T(8,128)(2,1)} %bitcast.65), custom_call_target="tpu_custom_call" | custom-call | tf_op jit(solution)/shard_map/pallas_call | solution.py:106
  88.8 1.9 %convolution_convert_fusion = bf16[512,256]{1,0:T(8,128)(2,1)S(1)} fusion(bf16[512,1024]{1,0:T(8,128)(2,1)} %bitcast.56, bf16[1024,256]{1,0:T(8,128)(2,1)} %bitcast.57), kind=kOutput, calls=%fused_computation.12 | convolution fusion | flops 268566528 | bytes 1835008 | tf_op jit(solution)/shard_map/dot_general | solution.py:501
  90.8 0.7 convolution_bitcast_fusion
  91.5 3.4 %copy-done.2 = bf16[8192,512]{1,0:T(8,128)(2,1)S(1)} copy-done((bf16[8192,512]{1,0:T(8,128)(2,1)S(1)}, bf16[8192,512]{1,0:T(8,128)(2,1)}, u32[]{:S(2)}) %copy-start.2) | copy-done | bytes 8388632
  94.9 35.4 %shard_map.159 = f32[8,8192]{1,0:T(8,128)S(1)} custom-call(s32[8192]{0:T(1024)S(1)} %get-tuple-element.15.idx_ref, s32[32,4]{1,0:T(8,128)S(1)} %broadcast_add_fusion.near_ref, f32[8200,128]{1,0:T(8,128)S(1)} %copy-done.4, f32[32,8,256]{2,1,0:T(8,128)S(1)} %get-tuple-element.11.lanes_ref, bf16[32,32,256]{2,1,0:T(8,128)(2,1)S(1)} %get-tuple-element.12.parts_ref, ...), custom_call_target="tpu_custom_call" | custom-call | tf_op jit(solution)/shard_map/pallas_call | solution.py:412
  130.3 12.0 %all_to_all.23 = f32[3,32,256]{2,0,1:T(4,128)S(1)} all-to-all(f32[3,32,256]{2,0,1:T(4,128)S(1)} %bitcast.59), channel_id=1, replica_groups=mesh['age'=8,'box'=4] {'age','box'}, dimensions={1} | all-to-all | bytes 196608 | tf_op jit(solution)/shard_map/all_to_all | solution.py:516
  142.3 7.8 %shard_map.160 = f32[8,4096]{1,0:T(8,128)S(1)} custom-call(s32[4096]{0:T(1024)S(1)} %fusion.21.idx_ref, f32[8,8192]{1,0:T(8,128)S(1)} %pad.19.x_ref), custom_call_target="tpu_custom_call" | custom-call | tf_op jit(solution)/shard_map/pallas_call | solution.py:188
  150.2 0.6 slice.19
  (31 shorter events, 0.8 us)
Async XLA Ops:
  0.0 90.8 %copy-start = (bf16[16,256,256]{2,1,0:T(8,128)(2,1)S(1)}, bf16[16,256,256]{2,1,0:T(8,128)(2,1)}, u32[]{:S(2)}) copy-start(bf16[16,256,256]{2,1,0:T(8,128)(2,1)} %param.27) | copy-start | bytes 6291460
  0.0 44.5 %copy-start.8 = (bf16[128,128,1]{1,0,2:T(8,128)(2,1)S(1)}, bf16[128,128,1]{1,0,2:T(8,128)(2,1)}, u32[]{:S(2)}) copy-start(bf16[128,128,1]{1,0,2:T(8,128)(2,1)} %constant.56) | copy-start | bytes 98308
  0.0 44.3 %copy-start.7 = (bf16[64,64]{1,0:T(8,128)(2,1)S(1)}, bf16[64,64]{1,0:T(8,128)(2,1)}, u32[]{:S(2)}) copy-start(bf16[64,64]{1,0:T(8,128)(2,1)} %constant.47.clone) | copy-start | bytes 24580
  18.9 25.9 %copy-start.6 = (f32[3,32]{1,0:T(4,128)S(1)}, f32[3,32]{1,0:T(4,128)}, u32[]{:S(2)}) copy-start(f32[3,32]{1,0:T(4,128)} %center_ref.1) | copy-start | bytes 1156
  30.0 13.8 %all-to-all-start = ((f32[8,32,256]{2,0,1:T(8,128)}), f32[8,32,256]{2,0,1:T(8,128)S(1)}, u32[]{:S(2)}, u32[]{:S(2)}) async-start(f32[8,32,256]{2,0,1:T(8,128)} %bitcast.5), calls=%async_computation | async-start | bytes 524288 | tf_op jit(solution)/shard_map/all_to_all | solution.py:469
  37.9 6.9 %copy-start.5 = (bf16[48,256]{1,0:T(8,128)(2,1)S(1)}, bf16[48,256]{1,0:T(8,128)(2,1)}, u32[]{:S(2)}) copy-start(bf16[48,256]{1,0:T(8,128)(2,1)} %shard_map.156.freq_ref) | copy-start | bytes 73732
  69.7 3.2 %copy-start.1 = (bf16[8192,512]{1,0:T(8,128)(2,1)}, bf16[8192,512]{1,0:T(8,128)(2,1)S(1)}, u32[]{:S(2)}) copy-start(bf16[8192,512]{1,0:T(8,128)(2,1)S(1)} %get-tuple-element.13.wave_ref) | copy-start | bytes 25165828
  72.9 2.0 %copy-start.3 = (f32[8200,128]{1,0:T(8,128)}, f32[8200,128]{1,0:T(8,128)S(1)}, u32[]{:S(2)}) copy-start(f32[8200,128]{1,0:T(8,128)S(1)} %get-tuple-element.10.rows_ref) | copy-start | bytes 12595204
  88.8 2.7 %copy-start.4 = (f32[8200,128]{1,0:T(8,128)S(1)}, f32[8200,128]{1,0:T(8,128)}, u32[]{:S(2)}) copy-start(f32[8200,128]{1,0:T(8,128)} %copy-done.3) | copy-start | bytes 12595204
  91.5 3.4 %copy-start.2 = (bf16[8192,512]{1,0:T(8,128)(2,1)S(1)}, bf16[8192,512]{1,0:T(8,128)(2,1)}, u32[]{:S(2)}) copy-start(bf16[8192,512]{1,0:T(8,128)(2,1)} %copy-done.1) | copy-start | bytes 25165828

commit v3 on v2

--- a/solution.py
+++ b/solution.py
@@ -14,6 +14,7 @@
 inv_two_pi = 0.15915494309189535
 LANES = 128
 VMEM_LIMIT = 32 * 1024 * 1024
+SMALL_LIMIT = 6 * 1024 * 1024
 
 
 def cos_coefficients(degree):
@@ -113,9 +114,98 @@
             pltpu.SemaphoreType.DMA((copies,)),
         ],
         compiler_params=pltpu.CompilerParams(
-            collective_id=collective_id, has_side_effects=True
+            collective_id=collective_id, has_side_effects=True, vmem_limit_bytes=SMALL_LIMIT
         ),
     )(x)
+
+
+def exchange_body(n_box, n, x_ref, o_ref, send_sem, recv_sem):
+    me = lax.axis_index("age") * n_box + lax.axis_index("box")
+    barrier = pltpu.get_barrier_semaphore()
+
+    def place(other):
+        return {"age": other // n_box, "box": lax.rem(other, n_box)}
+
+    def greet(d, carry):
+        pl.semaphore_signal(
+            barrier,
+            inc=1,
+            device_id=place(lax.rem(me + d, n)),
+            device_id_type=pl.DeviceIdType.MESH,
+        )
+        return carry
+
+    lax.fori_loop(1, n, greet, 0)
+    o_ref[me] = x_ref[me]
+    pl.semaphore_wait(barrier, n - 1)
+
+    def copy(d):
+        other = lax.rem(me + d, n)
+        return pltpu.make_async_remote_copy(
+            src_ref=x_ref.at[other],
+            dst_ref=o_ref.at[me],
+            send_sem=send_sem.at[d - 1],
+            recv_sem=recv_sem.at[d - 1],
+            device_id=place(other),
+            device_id_type=pl.DeviceIdType.MESH,
+        )
+
+    def send(d, carry):
+        copy(d).start()
+        return carry
+
+    def finish(d, carry):
+        copy(d).wait()
+        return carry
+
+    lax.fori_loop(1, n, send, 0)
+    lax.fori_loop(1, n, finish, 0)
+
+
+def exchange(x, n_box, collective_id):
+    n = x.shape[0]
+    return pl.pallas_call(
+        functools.partial(exchange_body, n_box, n),
+        out_shape=jax.ShapeDtypeStruct(x.shape, x.dtype),
+        in_specs=[pl.BlockSpec(memory_space=pltpu.VMEM)],
+        out_specs=pl.BlockSpec(memory_space=pltpu.VMEM),
+        scratch_shapes=[
+            pltpu.SemaphoreType.DMA((n - 1,)),
+            pltpu.SemaphoreType.DMA((n - 1,)),
+        ],
+        compiler_params=pltpu.CompilerParams(
+            collective_id=collective_id, has_side_effects=True, vmem_limit_bytes=SMALL_LIMIT
+        ),
+    )(x)
+
+
+def load_lanes(ref, i):
+    if len(ref.shape) == 2:
+        return ref[:, pl.ds(pl.multiple_of(i * LANES, LANES), LANES)]
+    per = ref.shape[2]
+    if per >= LANES:
+        k = per // LANES
+        return ref[i // k, :, pl.ds(pl.multiple_of(lax.rem(i, k) * LANES, LANES), LANES)]
+    m = LANES // per
+    return jnp.concatenate([ref[i * m + u] for u in range(m)], axis=1)
+
+
+def store_lanes(ref, i, tile):
+    if len(ref.shape) == 2:
+        ref[:, pl.ds(pl.multiple_of(i * LANES, LANES), LANES)] = tile
+        return
+    per = ref.shape[2]
+    if per >= LANES:
+        k = per // LANES
+        ref[i // k, :, pl.ds(pl.multiple_of(lax.rem(i, k) * LANES, LANES), LANES)] = tile
+        return
+    m = LANES // per
+    for u in range(m):
+        ref[i * m + u] = tile[:, u * per : (u + 1) * per]
+
+
+def columns(ref):
+    return ref.shape[-1] if len(ref.shape) == 2 else ref.shape[0] * ref.shape[2]
 
 
 def lanes_to_rows(tile):
@@ -126,7 +216,7 @@
 def fill_rows(src_ref, rows_ref, count):
     def step(i, carry):
         at = pl.multiple_of(i * LANES, LANES)
-        rows_ref[pl.ds(at, LANES), :] = lanes_to_rows(src_ref[:, pl.ds(at, LANES)])
+        rows_ref[pl.ds(at, LANES), :] = lanes_to_rows(load_lanes(src_ref, i))
         return carry
 
     lax.fori_loop(0, count // LANES, step, 0, unroll=8)
@@ -135,7 +225,7 @@
 def take_lanes(rows_ref, out_ref, count):
     def step(i, carry):
         at = pl.multiple_of(i * LANES, LANES)
-        out_ref[:, pl.ds(at, LANES)] = rows_ref[pl.ds(at, LANES), :].T[: out_ref.shape[0]]
+        store_lanes(out_ref, i, rows_ref[pl.ds(at, LANES), :].T[:8])
         return carry
 
     lax.fori_loop(0, count // LANES, step, 0, unroll=8)
@@ -172,16 +262,16 @@
 
 
 def spread_body(idx_ref, x_ref, out_ref, rows, placed):
-    fill_rows(x_ref, rows, x_ref.shape[1])
+    fill_rows(x_ref, rows, columns(x_ref))
     zero_rows(placed)
-    scatter_rows(idx_ref, rows, placed, x_ref.shape[1])
-    take_lanes(placed, out_ref, out_ref.shape[1])
+    scatter_rows(idx_ref, rows, placed, columns(x_ref))
+    take_lanes(placed, out_ref, columns(out_ref))
 
 
 def collect_body(idx_ref, x_ref, out_ref, src, rows):
-    fill_rows(x_ref, src, x_ref.shape[1])
-    gather_rows(idx_ref, src, rows, out_ref.shape[1])
-    take_lanes(rows, out_ref, out_ref.shape[1])
+    fill_rows(x_ref, src, columns(x_ref))
+    gather_rows(idx_ref, src, rows, columns(out_ref))
+    take_lanes(rows, out_ref, columns(out_ref))
 
 
 def permute_call(body, idx, x, out_shape, scratch_rows):
@@ -296,9 +386,9 @@
     idx_ref, center_ref, x_ref, basis_ref, freq_ref,
     rows_ref, block_ref, wave_ref, lanes_ref, parts_ref, scattered,
 ):
-    fill_rows(x_ref, scattered, x_ref.shape[1])
+    fill_rows(x_ref, scattered, columns(x_ref))
     zero_rows(rows_ref)
-    scatter_rows(idx_ref, scattered, rows_ref, x_ref.shape[1])
+    scatter_rows(idx_ref, scattered, rows_ref, columns(x_ref))
 
     def step(b, carry):
         one_box(
@@ -363,15 +453,18 @@
 
     def whole_box(count):
         target = lanes_ref[b]
-        table = stack16(dir_ref[...] * exp_ref[b], 2)
-        contract = (((1,), (1,)), ((), ()))
-        far = lax.dot_general(
-            table, wave_ref[pl.ds(here, per_box), :coef], contract, preferred_element_type=jnp.float32
-        )
-        far = far + lax.dot_general(
-            table, wave_ref[pl.ds(here, per_box), coef:], contract, preferred_element_type=jnp.float32
-        )
-        far = far[0:8] + far[8:16]
+        weighted = dir_ref[...] * exp_ref[b]
+        weighted = jnp.concatenate(
+            [weighted, jnp.zeros((LANES - 8, weighted.shape[1]), jnp.float32)], axis=0
+        )
+        table = jnp.concatenate(split16(weighted.T, 2), axis=1).astype(jnp.bfloat16)
+        far = jnp.dot(
+            wave_ref[pl.ds(here, per_box), :coef], table, preferred_element_type=jnp.float32
+        )
+        far = far + jnp.dot(
+            wave_ref[pl.ds(here, per_box), coef:], table, preferred_element_type=jnp.float32
+        )
+        far = far[:, :LANES] + far[:, LANES:]
         sums = pair_sums(near_ref[b, 0], target)
         for v in range(1, count):
             sums = sums + pair_sums(near_ref[b, v], target)
@@ -379,11 +472,11 @@
         near = jnp.concatenate(
             [*cross_parts(sums[0:3], target[0:3]), jnp.zeros((5, per_box), jnp.float32)], axis=0
         ) - jnp.concatenate([sums[4:7], jnp.zeros((5, per_box), jnp.float32)], axis=0)
-        total = near * inv_four_pi + far
+        total = near * inv_four_pi
         for i in range(per_box // LANES):
-            out_ref[pl.ds(here + i * LANES, LANES), :] = lanes_to_rows(
-                total[:, i * LANES : (i + 1) * LANES]
-            )
+            out_ref[pl.ds(here + i * LANES, LANES), :] = far[
+                i * LANES : (i + 1) * LANES
+            ] + lanes_to_rows(total[:, i * LANES : (i + 1) * LANES])
 
     held = (near_ref[b, 0] >= 0).astype(jnp.int32)
     for v in range(1, near_count):
@@ -403,15 +496,15 @@
         return carry
 
     lax.fori_loop(0, lanes_ref.shape[0], step, 0)
-    gather_rows(idx_ref, vel, rows, out_ref.shape[1])
-    take_lanes(rows, out_ref, out_ref.shape[1])
-
-
-def velocity_call(idx, near, rows, lanes, parts, wave, exps, basis_dir):
+    gather_rows(idx_ref, vel, rows, columns(out_ref))
+    take_lanes(rows, out_ref, columns(out_ref))
+
+
+def velocity_call(idx, out_shape, near, rows, lanes, parts, wave, exps, basis_dir):
     slots = wave.shape[0]
     return pl.pallas_call(
         velocity_body,
-        out_shape=jax.ShapeDtypeStruct((8, slots), jnp.float32),
+        out_shape=jax.ShapeDtypeStruct(out_shape, jnp.float32),
         in_specs=[pl.BlockSpec(memory_space=pltpu.SMEM)] * 2
         + [pl.BlockSpec(memory_space=pltpu.VMEM)] * 6,
         out_specs=pl.BlockSpec(memory_space=pltpu.VMEM),
@@ -464,9 +557,9 @@
         [position, strength, label[None, :], jnp.zeros((1, node_count), jnp.float32)], axis=0
     )
     payload = permute_call(
-        spread_body, send_at, fields, (8, slots_total), (node_count, slots_total)
-    )
-    got = lax.all_to_all(payload, AXES, split_axis=1, concat_axis=1, tiled=True)
+        spread_body, send_at, fields, (groups, 8, per_peer), (node_count, slots_total)
+    )
+    got = exchange(payload, n_box, 2)
 
     hit_source = (m2l_source[:, :, None] == all_order[None, None, :]).astype(jnp.bfloat16)
     kind_hits = (
@@ -485,7 +578,7 @@
         axis=2,
     ) - 1
 
-    got_label = got[6].astype(jnp.int32) - 1
+    got_label = got[:, 6, :].reshape(-1).astype(jnp.int32) - 1
     live = got_label >= 0
     tile_at = jnp.where(
         live, got_label * per_box + ranks(got_label, box_local), slots_total
@@ -505,6 +598,7 @@
     )
     back = velocity_call(
         jnp.minimum(tile_at, slots_total - 1),
+        (groups, 8, per_peer),
         near_local,
         rows,
         lanes,
@@ -513,8 +607,7 @@
         expansions.reshape(box_local, 1, coef),
         dir_rows,
     )
-    returned = lax.all_to_all(back[:3], AXES, split_axis=1, concat_axis=1, tiled=True)
-    returned = jnp.pad(returned, ((0, 5), (0, 0)))
+    returned = exchange(back, n_box, 3)
     out = permute_call(
         collect_body, send_at, returned, (8, node_count), (slots_total, node_count)
     )

time: 152 us -> 146 us (0.961)
  Pallas kernels: 104 us -> 129 us
  blocking collectives: 12 us -> 0 us
  local copies, waits for them, and re-layouts: 15.2 us -> 3.71 us
  starting transfers between devices: 3.62 us -> 0 us
  waiting for transfers between devices: 2.64 us -> 0 us
    pallas_call x1 -> x3, Pallas kernels: 35.4 us -> 62.6 us  [the longest x1 37.6 us: velocity_call(): pl.pallas_call(velocity_body, out_shape=jax.ShapeDtypeStruct(out_shape, j...]
    all_to_all x1 -> x0, blocking collectives: 12 us -> none  [per_device(): lax.all_to_all(back[:3], AXES, split_axis=1, concat_axis=1, tiled=True)]
    unnamed x18 -> x10, local copies, waits for them, and re-layouts: 8.59 us -> 0.02 us
    all_to_all x1 -> x0, starting transfers between devices: 3.62 us -> none  [per_device(): got = lax.all_to_all(payload, AXES, split_axis=1, concat_axis=1, tiled=True)]
    all_to_all x1 -> x0, waiting for transfers between devices: 2.64 us -> none  [per_device(): got = lax.all_to_all(payload, AXES, split_axis=1, concat_axis=1, tiled=True)]
    pallas_call x2, Pallas kernels: 25.9 us -> 24 us  [gather_blocks(): pl.pallas_call(functools.partial(gather_body, n_age, n_box), out_shape=ja...]
  transfers between devices with their start and end apart: 1 -> 0, of which waited for: 1 -> 0; matrix products, arithmetic and copies ran while one was open for 4% -> 0% of each run, Pallas kernels for 1% -> 0%
where the time goes in v3:
time: 146 us; the launch traced here: 145 us
  Pallas kernels  129 us (88%)
  other arithmetic  6.5 us (4%)
  matrix products  5.79 us (4%)
  local copies, waits for them, and re-layouts  3.71 us (3%)
    pallas_call x1, Pallas kernels, velocity_call(): pl.pallas_call(velocity_body, out_shape=jax.ShapeDtypeStruct(out_shape, j...  37.6 us
    pallas_call x2, Pallas kernels, exchange(): pl.pallas_call(functools.partial(exchange_body, n_box, n), out_shape=jax....  25 us
    pallas_call x1, Pallas kernels, group_call(): pl.pallas_call(group_body, out_shape=(jax.ShapeDtypeStruct((slots + 8, LA...  24.9 us
    pallas_call x2, Pallas kernels, gather_blocks(): pl.pallas_call(functools.partial(gather_body, n_age, n_box), out_shape=ja...  24 us
    pallas_call x2, Pallas kernels, permute_call(): pl.pallas_call(body, out_shape=jax.ShapeDtypeStruct(out_shape, jnp.float3...  16.1 us
    reduce_sum x1, other arithmetic, per_device(): jnp.sum(jnp.where(node_box[None, :] == all_order[:, None], jnp.arange(box...  3.03 us

profile of v3, /device:TPU:0, one launch (start us, length us, event | category | flops | bytes accessed | tf_op | source)
XLA Modules:
  0.0 145.0 jit_solution(406421119835208263)
XLA Ops:
  0.0 0.8 pad_bitcast_fusion.x_ref
  0.8 0.1 pad.20.clone
  0.9 0.9 select_reduce_fusion.1
  1.8 0.7 maximum_multiply_fusion
  2.5 0.6 pad.14.x_ref
  3.1 0.7 pad.13.basis_ref.dir_ref
  3.8 0.1 copy.25
  3.9 11.4 %shard_map.154 = s32[8,4,1,128]{3,2,1,0:T(1,128)S(1)} custom-call(s32[1,128]{1,0:T(1,128)S(1)} %pad_bitcast_fusion.x_ref), custom_call_target="tpu_custom_call" | custom-call | tf_op jit(solution)/shard_map/pallas_call | solution.py:107
  15.4 0.1 eq.87
  15.5 3.0 %select_reduce_fusion = s32[4096]{0:T(1024)S(1)} fusion(s32[4096]{0:T(1024)} %param.18, s32[1024]{0:T(1024)S(1)} %eq.87), kind=kLoop, calls=%fused_computation | loop fusion | flops 12578816 | bytes 36864 | tf_op jit(solution)/shard_map/reduce_sum | solution.py:545
  18.6 0.2 convert_reduce_fusion.1
  18.8 0.8 fusion.32
  19.6 1.0 fusion.13
  20.7 0.1 add_convert_fusion
  20.8 1.3 shard_map.157.freq_ref
  22.1 1.0 maximum_maximum_fusion.x_ref
  23.0 8.2 %shard_map.155.x_ref = f32[32,8,256]{2,1,0:T(8,128)S(1)} custom-call(s32[4096]{0:T(1024)S(1)} %fusion.20.idx_ref, f32[8,4096]{1,0:T(8,128)S(1)} %maximum_maximum_fusion.x_ref), custom_call_target="tpu_custom_call" | custom-call | tf_op jit(solution)/shard_map/pallas_call | solution.py:278
  31.2 12.1 %shard_map.156.x_ref = f32[32,8,256]{2,1,0:T(8,128)S(1)} custom-call(f32[32,8,256]{2,1,0:T(8,128)S(1)} %shard_map.155.x_ref), custom_call_target="tpu_custom_call" | custom-call | tf_op jit(solution)/shard_map/pallas_call | solution.py:167
  43.3 0.4 convert_reduce_fusion
  43.7 0.8 fusion.31
  44.5 0.1 compare_reduce_fusion
  44.6 1.1 fusion.11
  45.8 0.9 fusion.7
  46.7 0.6 copy.27
  47.3 24.9 %shard_map.158 = (f32[8200,128]{1,0:T(8,128)S(1)}, f32[32,1,256]{2,1,0:T(1,128)S(1)}, bf16[8192,512]{1,0:T(8,128)(2,1)S(1)}, f32[32,8,256]{2,1,0:T(8,128)S(1)}, bf16[32,32,256]{2,1,0:T(8,128)(2,1)S(1)}) custom-call(s32[8192]{0:T(1024)S(1)} %get-tuple-element.16.idx_ref, f32[3,32]{1,0:T(4,128)S(1)} %copy-done.2, f32[32,8,256]{2,1,0:T(8,128)S(1)} %shard_map.156.x_ref, ...), custom_call_target="tpu_custom_call" | custom-call | tf_op jit(solution)/shard_map/pallas_call | solution.py:416
  72.2 12.5 %shard_map.159 = bf16[8,4,32,256]{3,2,1,0:T(8,128)(2,1)S(1)} custom-call(bf16[32,256]{1,0:T(8,128)(2,1)S(1)} %bitcast.52), custom_call_target="tpu_custom_call" | custom-call | tf_op jit(solution)/shard_map/pallas_call | solution.py:107
  84.8 0.4 convolution_convert_fusion
  85.2 0.7 convolution_bitcast_fusion
  86.0 37.6 %shard_map.160.x_ref = f32[32,8,256]{2,1,0:T(8,128)S(1)} custom-call(s32[8192]{0:T(1024)S(1)} %get-tuple-element.15.idx_ref, s32[32,4]{1,0:T(8,128)S(1)} %broadcast_add_fusion.near_ref, f32[8200,128]{1,0:T(8,128)S(1)} %get-tuple-element.10.rows_ref, f32[32,8,256]{2,1,0:T(8,128)S(1)} %get-tuple-element.11.lanes_ref, ...), custom_call_target="tpu_custom_call" | custom-call | tf_op jit(solution)/shard_map/pallas_call | solution.py:505
  123.5 12.9 %shard_map.161.x_ref = f32[32,8,256]{2,1,0:T(8,128)S(1)} custom-call(f32[32,8,256]{2,1,0:T(8,128)S(1)} %shard_map.160.x_ref), custom_call_target="tpu_custom_call" | custom-call | tf_op jit(solution)/shard_map/pallas_call | solution.py:167
  136.5 7.9 %shard_map.162 = f32[8,4096]{1,0:T(8,128)S(1)} custom-call(s32[4096]{0:T(1024)S(1)} %fusion.20.idx_ref, f32[32,8,256]{2,1,0:T(8,128)S(1)} %shard_map.161.x_ref), custom_call_target="tpu_custom_call" | custom-call | tf_op jit(solution)/shard_map/pallas_call | solution.py:278
  144.4 0.6 slice.12
  (20 shorter events, 0.3 us)
Async XLA Ops:
  0.0 85.2 %copy-start = (bf16[16,256,256]{2,1,0:T(8,128)(2,1)S(1)}, bf16[16,256,256]{2,1,0:T(8,128)(2,1)}, u32[]{:S(2)}) copy-start(bf16[16,256,256]{2,1,0:T(8,128)(2,1)} %param.27) | copy-start | bytes 6291460
  0.0 45.8 %copy-start.4 = (s32[32,32]{1,0:T(8,128)S(1)}, s32[32,32]{1,0:T(8,128)}, u32[]{:S(2)}) copy-start(s32[32,32]{1,0:T(8,128)} %param.23) | copy-start | bytes 12292
  0.0 45.8 %copy-start.3 = (s32[32,32]{1,0:T(8,128)S(1)}, s32[32,32]{1,0:T(8,128)}, u32[]{:S(2)}) copy-start(s32[32,32]{1,0:T(8,128)} %param.22) | copy-start | bytes 12292
  19.6 27.7 %copy-start.2 = (f32[3,32]{1,0:T(4,128)S(1)}, f32[3,32]{1,0:T(4,128)}, u32[]{:S(2)}) copy-start(f32[3,32]{1,0:T(4,128)} %center_ref.1) | copy-start | bytes 1156
  22.1 25.2 %copy-start.1 = (bf16[48,256]{1,0:T(8,128)(2,1)S(1)}, bf16[48,256]{1,0:T(8,128)(2,1)}, u32[]{:S(2)}) copy-start(bf16[48,256]{1,0:T(8,128)(2,1)} %shard_map.157.freq_ref) | copy-start | bytes 73732

commit v4 on v3

--- a/solution.py
+++ b/solution.py
@@ -453,18 +453,21 @@
 
     def whole_box(count):
         target = lanes_ref[b]
-        weighted = dir_ref[...] * exp_ref[b]
-        weighted = jnp.concatenate(
-            [weighted, jnp.zeros((LANES - 8, weighted.shape[1]), jnp.float32)], axis=0
-        )
-        table = jnp.concatenate(split16(weighted.T, 2), axis=1).astype(jnp.bfloat16)
-        far = jnp.dot(
-            wave_ref[pl.ds(here, per_box), :coef], table, preferred_element_type=jnp.float32
-        )
-        far = far + jnp.dot(
-            wave_ref[pl.ds(here, per_box), coef:], table, preferred_element_type=jnp.float32
-        )
-        far = far[:, :LANES] + far[:, LANES:]
+        table = stack16(dir_ref[...] * exp_ref[b], 2)
+        contract = (((1,), (1,)), ((), ()))
+        far = lax.dot_general(
+            table,
+            wave_ref[pl.ds(here, per_box), :coef],
+            contract,
+            preferred_element_type=jnp.float32,
+        )
+        far = far + lax.dot_general(
+            table,
+            wave_ref[pl.ds(here, per_box), coef:],
+            contract,
+            preferred_element_type=jnp.float32,
+        )
+        far = far[0:8] + far[8:16]
         sums = pair_sums(near_ref[b, 0], target)
         for v in range(1, count):
             sums = sums + pair_sums(near_ref[b, v], target)
@@ -472,11 +475,11 @@
         near = jnp.concatenate(
             [*cross_parts(sums[0:3], target[0:3]), jnp.zeros((5, per_box), jnp.float32)], axis=0
         ) - jnp.concatenate([sums[4:7], jnp.zeros((5, per_box), jnp.float32)], axis=0)
-        total = near * inv_four_pi
+        total = near * inv_four_pi + far
         for i in range(per_box // LANES):
-            out_ref[pl.ds(here + i * LANES, LANES), :] = far[
-                i * LANES : (i + 1) * LANES
-            ] + lanes_to_rows(total[:, i * LANES : (i + 1) * LANES])
+            out_ref[pl.ds(here + i * LANES, LANES), :] = lanes_to_rows(
+                total[:, i * LANES : (i + 1) * LANES]
+            )
 
     held = (near_ref[b, 0] >= 0).astype(jnp.int32)
     for v in range(1, near_count):

time: 146 us -> 143 us (0.979)
  Pallas kernels: 129 us -> 126 us
    pallas_call x2, Pallas kernels: 25 us -> 23.3 us  [exchange(): pl.pallas_call(functools.partial(exchange_body, n_box, n), out_shape=jax....]
where the time goes in v4:
time: 143 us; the launch traced here: 142 us
  Pallas kernels  126 us (88%)
  other arithmetic  6.5 us (5%)
  matrix products  5.79 us (4%)
  local copies, waits for them, and re-layouts  3.71 us (3%)
    pallas_call x1, Pallas kernels, velocity_call(): pl.pallas_call(velocity_body, out_shape=jax.ShapeDtypeStruct(out_shape, j...  36.2 us
    pallas_call x1, Pallas kernels, group_call(): pl.pallas_call(group_body, out_shape=(jax.ShapeDtypeStruct((slots + 8, LA...  24.9 us
    pallas_call x2, Pallas kernels, gather_blocks(): pl.pallas_call(functools.partial(gather_body, n_age, n_box), out_shape=ja...  24 us
    pallas_call x2, Pallas kernels, exchange(): pl.pallas_call(functools.partial(exchange_body, n_box, n), out_shape=jax....  23.3 us
    pallas_call x2, Pallas kernels, permute_call(): pl.pallas_call(body, out_shape=jax.ShapeDtypeStruct(out_shape, jnp.float3...  16.1 us
    reduce_sum x1, other arithmetic, per_device(): jnp.sum(jnp.where(node_box[None, :] == all_order[:, None], jnp.arange(box...  3.03 us

profile of v4, /device:TPU:0, one launch (start us, length us, event | category | flops | bytes accessed | tf_op | source)
XLA Modules:
  0.0 141.9 jit_solution(14910717898718062985)
XLA Ops:
  0.0 0.8 pad_bitcast_fusion.x_ref
  0.8 0.1 pad.20.clone
  0.9 0.9 select_reduce_fusion.1
  1.8 0.7 maximum_multiply_fusion
  2.5 0.6 pad.14.x_ref
  3.1 0.7 pad.13.basis_ref.dir_ref
  3.8 0.1 copy.25
  3.9 11.4 %shard_map.154 = s32[8,4,1,128]{3,2,1,0:T(1,128)S(1)} custom-call(s32[1,128]{1,0:T(1,128)S(1)} %pad_bitcast_fusion.x_ref), custom_call_target="tpu_custom_call" | custom-call | tf_op jit(solution)/shard_map/pallas_call | solution.py:107
  15.4 0.1 eq.87
  15.5 3.0 %select_reduce_fusion = s32[4096]{0:T(1024)S(1)} fusion(s32[4096]{0:T(1024)} %param.18, s32[1024]{0:T(1024)S(1)} %eq.87), kind=kLoop, calls=%fused_computation | loop fusion | flops 12578816 | bytes 36864 | tf_op jit(solution)/shard_map/reduce_sum | solution.py:548
  18.6 0.2 convert_reduce_fusion.1
  18.8 0.8 fusion.32
  19.6 1.0 fusion.13
  20.7 0.1 add_convert_fusion
  20.8 1.3 shard_map.157.freq_ref
  22.1 1.0 maximum_maximum_fusion.x_ref
  23.0 8.2 %shard_map.155.x_ref = f32[32,8,256]{2,1,0:T(8,128)S(1)} custom-call(s32[4096]{0:T(1024)S(1)} %fusion.20.idx_ref, f32[8,4096]{1,0:T(8,128)S(1)} %maximum_maximum_fusion.x_ref), custom_call_target="tpu_custom_call" | custom-call | tf_op jit(solution)/shard_map/pallas_call | solution.py:278
  31.2 12.1 %shard_map.156.x_ref = f32[32,8,256]{2,1,0:T(8,128)S(1)} custom-call(f32[32,8,256]{2,1,0:T(8,128)S(1)} %shard_map.155.x_ref), custom_call_target="tpu_custom_call" | custom-call | tf_op jit(solution)/shard_map/pallas_call | solution.py:167
  43.3 0.4 convert_reduce_fusion
  43.7 0.8 fusion.31
  44.5 0.1 compare_reduce_fusion
  44.6 1.1 fusion.11
  45.8 0.9 fusion.7
  46.7 0.6 copy.27
  47.3 24.9 %shard_map.158 = (f32[8200,128]{1,0:T(8,128)S(1)}, f32[32,1,256]{2,1,0:T(1,128)S(1)}, bf16[8192,512]{1,0:T(8,128)(2,1)S(1)}, f32[32,8,256]{2,1,0:T(8,128)S(1)}, bf16[32,32,256]{2,1,0:T(8,128)(2,1)S(1)}) custom-call(s32[8192]{0:T(1024)S(1)} %get-tuple-element.16.idx_ref, f32[3,32]{1,0:T(4,128)S(1)} %copy-done.2, f32[32,8,256]{2,1,0:T(8,128)S(1)} %shard_map.156.x_ref, ...), custom_call_target="tpu_custom_call" | custom-call | tf_op jit(solution)/shard_map/pallas_call | solution.py:416
  72.2 12.5 %shard_map.159 = bf16[8,4,32,256]{3,2,1,0:T(8,128)(2,1)S(1)} custom-call(bf16[32,256]{1,0:T(8,128)(2,1)S(1)} %bitcast.52), custom_call_target="tpu_custom_call" | custom-call | tf_op jit(solution)/shard_map/pallas_call | solution.py:107
  84.8 0.4 convolution_convert_fusion
  85.2 0.7 convolution_bitcast_fusion
  86.0 36.2 %shard_map.160.x_ref = f32[32,8,256]{2,1,0:T(8,128)S(1)} custom-call(s32[8192]{0:T(1024)S(1)} %get-tuple-element.15.idx_ref, s32[32,4]{1,0:T(8,128)S(1)} %broadcast_add_fusion.near_ref, f32[8200,128]{1,0:T(8,128)S(1)} %get-tuple-element.10.rows_ref, f32[32,8,256]{2,1,0:T(8,128)S(1)} %get-tuple-element.11.lanes_ref, ...), custom_call_target="tpu_custom_call" | custom-call | tf_op jit(solution)/shard_map/pallas_call | solution.py:508
  122.1 11.2 %shard_map.161.x_ref = f32[32,8,256]{2,1,0:T(8,128)S(1)} custom-call(f32[32,8,256]{2,1,0:T(8,128)S(1)} %shard_map.160.x_ref), custom_call_target="tpu_custom_call" | custom-call | tf_op jit(solution)/shard_map/pallas_call | solution.py:167
  133.4 7.9 %shard_map.162 = f32[8,4096]{1,0:T(8,128)S(1)} custom-call(s32[4096]{0:T(1024)S(1)} %fusion.20.idx_ref, f32[32,8,256]{2,1,0:T(8,128)S(1)} %shard_map.161.x_ref), custom_call_target="tpu_custom_call" | custom-call | tf_op jit(solution)/shard_map/pallas_call | solution.py:278
  141.3 0.6 slice.12
  (20 shorter events, 0.3 us)
Async XLA Ops:
  0.0 85.2 %copy-start = (bf16[16,256,256]{2,1,0:T(8,128)(2,1)S(1)}, bf16[16,256,256]{2,1,0:T(8,128)(2,1)}, u32[]{:S(2)}) copy-start(bf16[16,256,256]{2,1,0:T(8,128)(2,1)} %param.27) | copy-start | bytes 6291460
  0.0 45.8 %copy-start.4 = (s32[32,32]{1,0:T(8,128)S(1)}, s32[32,32]{1,0:T(8,128)}, u32[]{:S(2)}) copy-start(s32[32,32]{1,0:T(8,128)} %param.23) | copy-start | bytes 12292
  0.0 45.8 %copy-start.3 = (s32[32,32]{1,0:T(8,128)S(1)}, s32[32,32]{1,0:T(8,128)}, u32[]{:S(2)}) copy-start(s32[32,32]{1,0:T(8,128)} %param.22) | copy-start | bytes 12292
  19.6 27.7 %copy-start.2 = (f32[3,32]{1,0:T(4,128)S(1)}, f32[3,32]{1,0:T(4,128)}, u32[]{:S(2)}) copy-start(f32[3,32]{1,0:T(4,128)} %center_ref.1) | copy-start | bytes 1156
  22.1 25.2 %copy-start.1 = (bf16[48,256]{1,0:T(8,128)(2,1)S(1)}, bf16[48,256]{1,0:T(8,128)(2,1)}, u32[]{:S(2)}) copy-start(bf16[48,256]{1,0:T(8,128)(2,1)} %shard_map.157.freq_ref) | copy-start | bytes 73732
